TPU v7x, 32 devices: a whole 2x2x4 slice. The times are simulated.
32 devices in a mesh: dom: 8 (over z, y), rep: 4 (over x, core).
Axes of the slice: x: 2, y: 2, z: 4, core: 2. Of those that a mesh axis runs over, the one named last changes fastest.
Arguments:
- feats: bfloat16 [4096, 512], P('dom', 'rep'), may hold values from -6 to 6
- hist_one: bfloat16 [4096, 512], P('dom', 'rep'), may hold values from -6 to 6
- local_val: bfloat16 [4096, 128], P('dom'), may hold values from -0.375 to 0.375
- halo_val: bfloat16 [4096, 128], P('dom'), may hold values from -0.375 to 0.375
- halo_send: int32 [8, 8, 64], P('dom'), may hold values from 0 to 511
- halo_tile: int32 [8, 4], P('dom'), may hold values from 0 to 3, as said below
- tile_type: int32 [8, 4], P('dom'), may hold values from 0 to 7
- w_one: bfloat16 [512, 8, 512], P(None, None, 'rep'), may hold values from -0.25 to 0.25
- w_two: bfloat16 [512, 8, 512], P(None, None, 'rep'), may hold values from -0.25 to 0.25
- grad_out: bfloat16 [4096, 512], P('dom', 'rep'), may hold values from -6 to 6
Outputs:
- hidden_two: bfloat16 [4096, 512], P('dom', 'rep')
- history_one: bfloat16 [4096, 512], P('dom', 'rep')
- grad_w_one: float32 [512, 8, 512], P(None, None, 'rep')
- grad_w_two: float32 [512, 8, 512], P(None, None, 'rep')
Inputs may be any that keep to these rules, and one draw needn't show every extreme that they name: `halo_tile`: for each partition, every one of the 4 halo blocks is read by exactly 1 of its row blocks.
All inputs are finite; a program needn't handle non-finite values.
Results may differ from a plain program's by a relative error of at most 0.013.
Values may be sent and summed in bfloat16 or wider, within the bound.
A program may use at most 64 MiB of HBM per device.

v0:
```python
import jax
import jax.numpy as jnp
from jax import lax
from jax.sharding import PartitionSpec as P


def slope_silu(value):
    sig = jax.nn.sigmoid(value)
    return sig * (1.0 + value * (1.0 - sig))


def pull_rows(table, send_rows):
    picked = jnp.take(table, send_rows, axis=0)
    landed = lax.all_to_all(picked, "dom", split_axis=0, concat_axis=0, tiled=True)
    return landed.reshape(-1, table.shape[1])


def aggregate(source, halo, local_blocks, halo_blocks, halo_pick):
    rows, tile, _ = local_blocks.shape
    width = source.shape[1]
    src = source.reshape(rows, tile, width)
    halo_tiles = jnp.take(halo.reshape(-1, tile, width), halo_pick, axis=0)
    total = jnp.einsum("jrk,jkc->jrc", local_blocks, src, preferred_element_type=jnp.float32)
    total = total + jnp.einsum(
        "jrk,jkc->jrc", halo_blocks, halo_tiles, preferred_element_type=jnp.float32
    )
    return total.astype(jnp.bfloat16)


def mix_layer(source, halo, local_blocks, halo_blocks, halo_pick):
    whole_source, whole_halo = (
        lax.all_gather(source, "rep", axis=1, tiled=True),
        lax.all_gather(halo, "rep", axis=1, tiled=True),
    )
    return aggregate(whole_source, whole_halo, local_blocks, halo_blocks, halo_pick)


def expert_forward(agg_full, weights, types):
    chosen = jnp.take(weights, types, axis=1)
    return jnp.einsum("jrd,djc->jrc", agg_full, chosen, preferred_element_type=jnp.float32)


def grad_term(agg_full, dz_rows, onehot):
    per_tile = jnp.einsum("jrd,jrc->jdc", agg_full, dz_rows, preferred_element_type=jnp.float32)
    return jnp.einsum("je,jdc->dec", onehot, per_tile)


def shards(
    feats, hist_one, local_val, halo_val, halo_send, halo_tile, tile_type, w_one, w_two, grad_out
):
    tile = local_val.shape[1]
    rows = feats.shape[0] // tile
    cols = feats.shape[1]
    experts = w_one.shape[1]
    local_blocks = local_val.reshape(rows, tile, tile)
    halo_blocks = halo_val.reshape(rows, tile, tile)
    halo_pick = halo_tile[0]
    types = tile_type[0]
    send_rows = halo_send[0]
    halo_first = pull_rows(feats, send_rows)
    agg_one = mix_layer(feats, halo_first, local_blocks, halo_blocks, halo_pick)
    z_one = expert_forward(agg_one, w_one, types)
    h_one = (feats.reshape(rows, tile, cols).astype(jnp.float32) + jax.nn.silu(z_one)).astype(
        jnp.bfloat16
    )
    halo_second = pull_rows(hist_one, send_rows)
    agg_two = mix_layer(h_one.reshape(-1, cols), halo_second, local_blocks, halo_blocks, halo_pick)
    z_two = expert_forward(agg_two, w_two, types)
    h_two = (h_one.astype(jnp.float32) + jax.nn.silu(z_two)).astype(jnp.bfloat16)
    onehot = (types[:, None] == jnp.arange(experts, dtype=jnp.int32)[None, :]).astype(jnp.float32)
    upstream = grad_out.reshape(rows, tile, cols).astype(jnp.float32)
    dz_two = (upstream * slope_silu(z_two)).astype(jnp.bfloat16)
    chosen_two = jnp.take(w_two, types, axis=1)
    partial_back = jnp.einsum(
        "jrc,djc->jrd", dz_two, chosen_two, preferred_element_type=jnp.float32
    )
    own_cols = lax.psum_scatter(
        partial_back.astype(jnp.bfloat16), "rep", scatter_dimension=2, tiled=True
    )
    dh_one = upstream + jnp.einsum(
        "jrk,jrc->jkc", local_blocks, own_cols, preferred_element_type=jnp.float32
    )
    dz_one = (dh_one * slope_silu(z_one)).astype(jnp.bfloat16)
    grad_one, grad_two = lax.psum(
        (grad_term(agg_one, dz_one, onehot), grad_term(agg_two, dz_two, onehot)), "dom"
    )
    return (h_two.reshape(-1, cols), h_one.reshape(-1, cols), grad_one, grad_two)


def solution(mesh):
    in_specs = (
        P("dom", "rep"),
        P("dom", "rep"),
        P("dom", None),
        P("dom", None),
        P("dom", None, None),
        P("dom", None),
        P("dom", None),
        P(None, None, "rep"),
        P(None, None, "rep"),
        P("dom", "rep"),
    )
    out_specs = (P("dom", "rep"), P("dom", "rep"), P(None, None, "rep"), P(None, None, "rep"))
    return jax.shard_map(shards, mesh=mesh, in_specs=in_specs, out_specs=out_specs, check_vma=False)
```

profile of v0, /device:TPU:0, one launch (start us, length us, event | category | flops | bytes accessed | tf_op | source)
XLA Modules:
  0.0 268.8 jit_solution(15571073136750010894)
XLA Ops:
  7.2 0.0 copy-start
  7.2 0.0 copy-start.2
  7.2 0.8 compare_and_fusion
  8.0 0.7 compare_select_fusion
  8.7 0.1 reshape.129
  8.8 2.0 gather_fusion.3
  10.8 2.0 gather_fusion
  12.7 0.8 broadcast_select_fusion
  13.6 7.3 %all-to-all-start = ((bf16[8,64,128]{2,1,0:T(8,128)(2,1)}), bf16[8,64,128]{2,1,0:T(8,128)(2,1)S(1)}, u32[]{:S(2)}, u32[]{:S(2)}) async-start(bf16[8,64,128]{2,1,0:T(8,128)(2,1)} %get-tuple-element.10), calls=%async_computation | async-start | bytes 262144 | tf_op jit(solution)/shard_map/all_to_all | solution.py:14
  20.9 7.6 %all_gather.12 = bf16[512,512]{1,0:T(8,128)(2,1)} all-gather(bf16[512,128]{1,0:T(8,128)(2,1)S(1)} %copy-done.2), channel_id=1, replica_groups=mesh['dom'=8,'rep'=4] {'rep'}, dimensions={1}, use_global_device_ids=true | all-gather | bytes 655360 | tf_op jit(solution)/shard_map/all_gather | solution.py:32
  28.6 0.0 copy-start.1
  28.6 2.9 %gather_fusion.5 = bf16[4,512,128]{2,0,1:T(4,128)(2,1)S(1)} fusion(bf16[512,8,128]{2,1,0:T(8,128)(2,1)S(1)} %copy-done, s32[1024]{0:T(1024)S(1)} %pad_clamp_fusion), kind=kCustom, calls=%fused_computation.5.clone | custom fusion | bytes 1048592 | tf_op jit(solution)/shard_map/jit(_take)/gather | solution.py:39
  31.5 2.9 %gather_fusion.2 = bf16[4,512,128]{2,0,1:T(4,128)(2,1)S(1)} fusion(bf16[512,8,128]{2,1,0:T(8,128)(2,1)S(1)} %copy-done.1, s32[1024]{0:T(1024)S(1)} %pad_clamp_fusion), kind=kCustom, calls=%fused_computation.2.clone | custom fusion | bytes 1048592 | tf_op jit(solution)/shard_map/jit(_take)/gather | solution.py:39
  34.5 1.3 fusion.41
  35.8 1.5 select_bitcast_fusion
  37.3 6.1 %all-to-all-start.1 = ((bf16[8,64,128]{2,1,0:T(8,128)(2,1)}), bf16[8,64,128]{2,1,0:T(8,128)(2,1)S(1)}, u32[]{:S(2)}, u32[]{:S(2)}) async-start(bf16[8,64,128]{2,1,0:T(8,128)(2,1)} %get-tuple-element.9), calls=%async_computation.1 | async-start | bytes 262144 | tf_op jit(solution)/shard_map/all_to_all | solution.py:14
  43.5 0.0 reduce-scatter.4.cloned.1.call-start
  43.5 7.0 %all_gather.13 = bf16[512,512]{1,0:T(8,128)(2,1)S(1)} all-gather(bf16[512,128]{1,0:T(8,128)(2,1)S(1)} %bitcast.82), channel_id=1, replica_groups=mesh['dom'=8,'rep'=4] {'rep'}, dimensions={1}, use_global_device_ids=true | all-gather | bytes 655360 | tf_op jit(solution)/shard_map/all_gather | solution.py:33
  50.6 0.4 all-to-all-done.1
  51.0 7.4 %all_gather.15 = bf16[512,512]{1,0:T(8,128)(2,1)} all-gather(bf16[512,128]{1,0:T(8,128)(2,1)S(1)} %bitcast.83), channel_id=1, replica_groups=mesh['dom'=8,'rep'=4] {'rep'}, dimensions={1}, use_global_device_ids=true | all-gather | bytes 655360 | tf_op jit(solution)/shard_map/all_gather | solution.py:33
  58.3 0.6 gather_fusion.1
  58.9 1.6 gather_fusion.4
  60.6 0.0 copy-start.7
  60.6 0.4 fusion.2
  61.0 0.0 copy-start.10
  61.0 0.6 copy-done.7
  61.6 0.3 fusion.20
  61.9 7.3 %all_gather.14 = bf16[512,512]{1,0:T(8,128)(2,1)S(1)} all-gather(bf16[512,128]{1,0:T(8,128)(2,1)S(1)} %bitcast.89), channel_id=1, replica_groups=mesh['dom'=8,'rep'=4] {'rep'}, dimensions={1}, use_global_device_ids=true | all-gather | bytes 655360 | tf_op jit(solution)/shard_map/all_gather | solution.py:32
  69.3 0.3 fusion.42
  69.6 0.4 fusion.1
  70.1 0.2 copy-done.4
  70.3 1.0 add_convert_fusion
  71.3 0.7 copy-done.15
  72.0 0.3 convolution_convert_fusion
  72.3 0.3 copy.46
  72.7 0.9 copy.67
  73.5 0.0 reduce-scatter.4.cloned.1.call-update
  73.6 0.0 all-reduce.3.cloned.1.call-start
  73.6 1.3 fusion.38
  75.0 1.9 convolution_bitcast_fusion
  76.9 19.1 %reduce-scatter.4.cloned.1.call-done = bf16[128,512]{1,0:T(8,128)(2,1)} async-done(((bf16[512,512]{1,0:T(8,128)(2,1)}), bf16[128,512]{1,0:T(8,128)(2,1)}) %reduce-scatter.4.cloned.1.call-update) | async-done | bytes 131088
  95.9 0.9 reshape.147
  96.9 0.5 fusion.6
  97.4 1.9 convolution_bitcast_fusion.1
  99.3 0.0 all-reduce.3.cloned.1.call-update
  99.3 158.1 %all-reduce.3.cloned.1.call-done = (f32[512,8,128]{2,1,0:T(8,128)}, f32[512,8,128]{2,1,0:T(8,128)}) async-done(((f32[512,8,128]{2,1,0:T(8,128)}, f32[512,8,128]{2,1,0:T(8,128)}), (f32[512,8,128]{2,1,0:T(8,128)}, f32[512,8,128]{2,1,0:T(8,128)})) %all-reduce.3.cloned.1.call-update) | async-done | bytes 4194320 | tf_op jit(solution)/shard_map/psum | solution.py:84
  257.4 3.2 %copy.70 = f32[512,8,128]{2,1,0:T(8,128)} copy(f32[512,8,128]{2,1,0:T(8,128)} %get-tuple-element.19) | data formatting | bytes 4194304
  260.6 1.3 copy.71
  (32 shorter events, 0.1 us)
Async XLA Ops:
  7.2 21.4 %copy-start = (bf16[512,8,128]{2,1,0:T(8,128)(2,1)S(1)}, bf16[512,8,128]{2,1,0:T(8,128)(2,1)}, u32[]{:S(2)}) copy-start(bf16[512,8,128]{2,1,0:T(8,128)(2,1)} %param.24) | copy-start | bytes 3145732
  7.2 13.7 %copy-start.2 = (bf16[512,128]{1,0:T(8,128)(2,1)S(1)}, bf16[512,128]{1,0:T(8,128)(2,1)}, u32[]{:S(2)}) copy-start(bf16[512,128]{1,0:T(8,128)(2,1)} %param.16) | copy-start | bytes 393220
  7.2 13.7 %copy-start.12 = (s32[1,4]{1,0:T(1,128)S(1)}, s32[1,4]{1,0:T(1,128)}, u32[]{:S(2)}) copy-start(s32[1,4]{1,0:T(1,128)} %param.22) | copy-start | bytes 52
  13.6 23.7 %all-to-all-start = ((bf16[8,64,128]{2,1,0:T(8,128)(2,1)}), bf16[8,64,128]{2,1,0:T(8,128)(2,1)S(1)}, u32[]{:S(2)}, u32[]{:S(2)}) async-start(bf16[8,64,128]{2,1,0:T(8,128)(2,1)} %get-tuple-element.10), calls=%async_computation | async-start | bytes 262144 | tf_op jit(solution)/shard_map/all_to_all | solution.py:14
  28.6 3.0 %copy-start.1 = (bf16[512,8,128]{2,1,0:T(8,128)(2,1)S(1)}, bf16[512,8,128]{2,1,0:T(8,128)(2,1)}, u32[]{:S(2)}) copy-start(bf16[512,8,128]{2,1,0:T(8,128)(2,1)} %param.23) | copy-start | bytes 3145732
  31.5 3.0 %copy-start.9 = (bf16[512,128]{1,0:T(8,128)(2,1)S(1)}, bf16[512,128]{1,0:T(8,128)(2,1)}, u32[]{:S(2)}) copy-start(bf16[512,128]{1,0:T(8,128)(2,1)} %param.18) | copy-start | bytes 393220
  34.5 2.8 %copy-start.14 = (s32[1,4]{1,0:T(1,128)S(1)}, s32[1,4]{1,0:T(1,128)}, u32[]{:S(2)}) copy-start(s32[1,4]{1,0:T(1,128)} %param.21) | copy-start | bytes 52
  37.3 23.3 %copy-start.8 = (bf16[512,128]{1,0:T(8,128)(2,1)S(1)}, bf16[512,128]{1,0:T(8,128)(2,1)}, u32[]{:S(2)}) copy-start(bf16[512,128]{1,0:T(8,128)(2,1)} %param.19) | copy-start | bytes 393220
  37.3 13.6 %all-to-all-start.1 = ((bf16[8,64,128]{2,1,0:T(8,128)(2,1)}), bf16[8,64,128]{2,1,0:T(8,128)(2,1)S(1)}, u32[]{:S(2)}, u32[]{:S(2)}) async-start(bf16[8,64,128]{2,1,0:T(8,128)(2,1)} %get-tuple-element.9), calls=%async_computation.1 | async-start | bytes 262144 | tf_op jit(solution)/shard_map/all_to_all | solution.py:14
  43.5 52.5 %reduce-scatter.4.cloned.1.call-start = ((), (), s32[]{:S(2)}) async-start(), calls=%async_computation.3 | async-start | bytes 655360
  60.6 1.0 copy-start.7
  61.0 1.0 copy-start.5
  61.0 8.3 %copy-start.10 = (bf16[512,128]{1,0:T(8,128)(2,1)S(1)}, bf16[512,128]{1,0:T(8,128)(2,1)}, u32[]{:S(2)}) copy-start(bf16[512,128]{1,0:T(8,128)(2,1)} %param.18) | copy-start | bytes 393220
  61.9 8.1 %copy-start.11 = (bf16[4,128,128]{2,1,0:T(8,128)(2,1)}, bf16[4,128,128]{2,1,0:T(8,128)(2,1)S(1)}, u32[]{:S(2)}) copy-start(bf16[4,128,128]{2,1,0:T(8,128)(2,1)S(1)} %get-tuple-element.13) | copy-start | bytes 393220
  69.2 1.0 copy-start.4
  69.6 2.4 copy-start.13
  71.3 0.7 copy-start.15
  73.6 23.3 %copy-start.6 = (bf16[4,128,512]{2,1,0:T(8,128)(2,1)S(1)}, bf16[4,128,512]{2,1,0:T(8,128)(2,1)}, u32[]{:S(2)}) copy-start(bf16[4,128,512]{2,1,0:T(8,128)(2,1)} %copy-done.5) | copy-start | bytes 1572868
  73.6 183.8 %all-reduce.3.cloned.1.call-start = ((), (), s32[]{:S(2)}) async-start(), calls=%async_computation.4 | async-start | bytes 8388608 | tf_op jit(solution)/shard_map/psum | solution.py:84
  257.4 3.2 %copy-start.3 = (f32[512,8,128]{2,1,0:T(8,128)S(1)}, f32[512,8,128]{2,1,0:T(8,128)}, u32[]{:S(2)}) copy-start(f32[512,8,128]{2,1,0:T(8,128)} %get-tuple-element.20) | copy-start | bytes 6291460
Sparse Core Ops, SparseCore 0:
  73.7 22.2 reduce-scatter.3
  100.7 156.6 all-reduce.2
where the time goes:
time: 269 us
  waiting for transfers between devices  178 us (66%)
  blocking collectives  29.4 us (11%)
  local copies, waits for them, and re-layouts  20.4 us (8%)
  between operations  14.4 us (5%)
  starting transfers between devices  13.5 us (5%)
  matrix products  9.75 us (4%)
  other arithmetic  3.85 us (1%)
    psum x1, waiting for transfers between devices, shards(): lax.psum((grad_term(agg_one, dz_one, onehot), grad_term(agg_two, dz_two,...  158 us
    unnamed x3, waiting for transfers between devices  19.1 us
    all_gather x2, blocking collectives, mix_layer(): lax.all_gather(source, 'rep', axis=1, tiled=True)  15 us
    all_gather x2, blocking collectives, mix_layer(): lax.all_gather(halo, 'rep', axis=1, tiled=True)  14.4 us
    all_to_all x2, starting transfers between devices, pull_rows(): lax.all_to_all(picked, 'dom', split_axis=0, concat_axis=0, tiled=True)  13.4 us
    unnamed x37, local copies, waits for them, and re-layouts  8.27 us
    gather x2, local copies, waits for them, and re-layouts, expert_forward(): chosen = jnp.take(weights, types, axis=1)  5.86 us
  transfers between devices with their start and end apart: 4, of which 3 were waited for; matrix products, arithmetic and copies ran while one was open for 4% of the time, Pallas kernels for 0%

commit v1 on v0

v1 whole, which is shorter than its diff:
```python
import functools

import jax
import jax.numpy as jnp
from jax import lax
from jax.experimental import pallas as pl
from jax.experimental.pallas import tpu as pltpu
from jax.sharding import PartitionSpec as P

MESH = pl.DeviceIdType.MESH
BF = jnp.bfloat16
F32 = jnp.float32
STREAMS = 2


def sigmoid(value):
    return 1.0 / (1.0 + jnp.exp(-value))


def slope_silu(value):
    sig = sigmoid(value)
    return sig * (1.0 + value * (1.0 - sig))


def dot(a, b, dims=((1,), (0,))):
    return lax.dot_general(a, b, (dims, ((), ())), preferred_element_type=F32)


def bit_orders(n_dom):
    bits = list(range(n_dom.bit_length() - 1))
    swapped = [bits[1], bits[0]] + bits[2:] if len(bits) > 1 else bits
    return [bits, swapped][:STREAMS]


def step_kernel(
    n_dom, n_rep, cap, tile,
    feats, hist, lval, hval, picks, htile, types, w1, w2, gout,
    h2_out, h1_out, res1, res2,
    picked, halo, agg1, agg2, pbs, pbr, z1s, dzm, spread_halo, acc, sbuf, rbuf,
    pick_send, pick_recv, ag_send, ag_recv, pb_send, pb_recv, rs_send, rs_recv, gat_send, gat_recv,
):
    nodes, cols = feats.shape
    rows = nodes // tile
    width = agg1.shape[1]
    experts = dzm.shape[1] // cols
    pad = picked.shape[1] // n_dom
    me = lax.axis_index("dom")
    mr = lax.axis_index("rep")
    barrier = pltpu.get_barrier_semaphore()

    def greet_dom(k, carry):
        pl.semaphore_signal(
            barrier, inc=1, device_id={"dom": (me + k) % n_dom}, device_id_type=MESH
        )
        return carry

    lax.fori_loop(1, n_dom, greet_dom, 0)
    for k in range(1, n_rep):
        pl.semaphore_signal(
            barrier, inc=1, device_id={"rep": (mr + k) % n_rep}, device_id_type=MESH
        )

    onehot = (
        picks[...] == lax.broadcasted_iota(jnp.int32, (n_dom * pad, nodes), 1)
    ).astype(F32).astype(BF)
    picked[0] = dot(onehot, feats[...]).astype(BF)
    picked[1] = dot(onehot, hist[...]).astype(BF)
    pl.semaphore_wait(barrier, n_dom - 1 + n_rep - 1)

    def pick_copy(layer, k):
        to = (me + k) % n_dom
        return pltpu.make_async_remote_copy(
            src_ref=picked.at[layer, pl.ds(pl.multiple_of(to * pad, pad), pad)],
            dst_ref=halo.at[layer, pl.ds(pl.multiple_of(me * pad, pad), pad)],
            send_sem=pick_send.at[layer, k],
            recv_sem=pick_recv.at[layer, k],
            device_id={"dom": to},
            device_id_type=MESH,
        )

    def loop_picks(layer, act):
        def body(k, carry):
            act(pick_copy(layer, k))
            return carry

        lax.fori_loop(1, n_dom, body, 0)

    own = pl.ds(pl.multiple_of(me * pad, pad), pad)
    for layer in range(2):
        loop_picks(layer, lambda copy: copy.start())
        halo[layer, own] = picked[layer, own]

    def compact(layer):
        if pad == cap:
            return
        total = n_dom * cap
        r = lax.broadcasted_iota(jnp.int32, (total, n_dom * pad), 0)
        c = lax.broadcasted_iota(jnp.int32, (total, n_dom * pad), 1)
        chosen = ((r // cap) * pad + r % cap == c).astype(F32).astype(BF)
        halo[layer, pl.ds(0, total)] = dot(chosen, halo[layer]).astype(BF)

    def block(j):
        return pl.ds(j * tile, tile)

    def own_cols(r):
        return pl.ds(pl.multiple_of(r * cols, cols), cols)

    def ag_copy(layer, k):
        part = (agg1, agg2)[layer].at[:, own_cols(mr)]
        return pltpu.make_async_remote_copy(
            src_ref=part,
            dst_ref=part,
            send_sem=ag_send.at[layer, k],
            recv_sem=ag_recv.at[layer, k],
            device_id={"rep": (mr + k) % n_rep},
            device_id_type=MESH,
        )

    def aggregate(layer, source):
        full = (agg1, agg2)[layer]
        local = [dot(lval[block(j)], source[block(j)]) for j in range(rows)]
        loop_picks(layer, lambda copy: copy.wait_recv())
        compact(layer)
        for j in range(rows):
            there = dot(spread_halo[block(j)], halo[layer, pl.ds(0, n_dom * cap)])
            full[block(j), own_cols(mr)] = (local[j] + there).astype(BF)
        for k in range(1, n_rep):
            ag_copy(layer, k).start()
        for k in range(1, n_rep):
            ag_copy(layer, k).wait_recv()

    for b in range(n_dom * cap // tile):
        held = (htile[...] == b).astype(F32)
        spread_halo[:, b * tile : (b + 1) * tile] = (hval[...].astype(F32) * held).astype(BF)

    aggregate(0, feats)
    for j in range(rows):
        z = dot(agg1[block(j)], w1[j])
        z1s[block(j)] = z
        h1_out[block(j)] = (feats[block(j)].astype(F32) + z * sigmoid(z)).astype(BF)

    aggregate(1, h1_out)

    def spread_types(j, dz):
        for t in range(experts):
            held = (types[block(j)] == t).astype(F32)
            dzm[block(j), t * cols : (t + 1) * cols] = (dz * held).astype(BF)

    for j in range(rows):
        z = dot(agg2[block(j)], w2[j])
        h2_out[block(j)] = (h1_out[block(j)].astype(F32) + z * sigmoid(z)).astype(BF)
        dz = gout[block(j)].astype(F32) * slope_silu(z)
        spread_types(j, dz)
        back = dot(dz.astype(BF), w2[j], ((1,), (1,))).astype(BF)
        for r in range(n_rep):
            pbs[r, block(j)] = back[:, r * cols : (r + 1) * cols]

    def pb_copy(k):
        to = (mr + k) % n_rep
        return pltpu.make_async_remote_copy(
            src_ref=pbs.at[to],
            dst_ref=pbr.at[k],
            send_sem=pb_send.at[k],
            recv_sem=pb_recv.at[k],
            device_id={"rep": to},
            device_id_type=MESH,
        )

    for k in range(1, n_rep):
        pb_copy(k).start()

    orders = bit_orders(n_dom)
    streams = len(orders)
    length = acc.shape[2]
    sub = width // streams
    results = (res1, res2)

    def my_bit(b):
        return (me // (1 << b)) % 2

    def partner(b):
        return me + (1 - 2 * my_bit(b)) * (1 << b)

    def base(q, step):
        start = 0
        for s in range(step):
            start = start + my_bit(orders[q][s]) * (length >> (s + 1))
        return start

    def span(start, size):
        return pl.ds(pl.multiple_of(start, size), size)

    def rs_copy(layer, q, s):
        b, half = orders[q][s], length >> (s + 1)
        gone = span(base(q, s) + (1 - my_bit(b)) * half, half)
        return pltpu.make_async_remote_copy(
            src_ref=sbuf.at[layer, q, gone],
            dst_ref=rbuf.at[layer, q, pl.ds(length - (length >> s), half)],
            send_sem=rs_send.at[layer, q, s],
            recv_sem=rs_recv.at[layer, q, s],
            device_id={"dom": partner(b)},
            device_id_type=MESH,
        )

    def gat_copy(layer, q, s):
        b, size = orders[q][s], length >> (s + 1)
        part = results[layer].at[q, span(base(q, s + 1), size)]
        return pltpu.make_async_remote_copy(
            src_ref=part,
            dst_ref=part,
            send_sem=gat_send.at[layer, q, s],
            recv_sem=gat_recv.at[layer, q, s],
            device_id={"dom": partner(b)},
            device_id_type=MESH,
        )

    def rs_send_half(layer, q, s):
        b, half = orders[q][s], length >> (s + 1)
        gone = span(base(q, s) + (1 - my_bit(b)) * half, half)
        sbuf[layer, q, gone] = acc[layer, q, gone].astype(BF)
        rs_copy(layer, q, s).start()

    def rs_begin(layer):
        agg = (agg1, agg2)[layer]
        for q in range(streams):
            grad = dot(agg[:, q * sub : (q + 1) * sub], dzm[...], ((0,), (0,)))
            for t in range(experts):
                acc[layer, q, t * sub : (t + 1) * sub] = grad[:, t * cols : (t + 1) * cols]
            rs_send_half(layer, q, 0)

    depth = len(orders[0])

    def rs_step(layer, s):
        for q in range(streams):
            half = length >> (s + 1)
            kept = span(base(q, s + 1), half)
            rs_copy(layer, q, s).wait_recv()
            got = rbuf[layer, q, pl.ds(length - (length >> s), half)].astype(F32)
            if s + 1 < depth:
                acc[layer, q, kept] += got
                rs_send_half(layer, q, s + 1)
            else:
                results[layer][q, kept] = (acc[layer, q, kept] + got).astype(BF)
                gat_copy(layer, q, s).start()

    def gat_step(layer, s):
        for q in range(streams):
            gat_copy(layer, q, s).wait_recv()
            if s > 0:
                gat_copy(layer, q, s - 1).start()

    rs_begin(1)

    for k in range(1, n_rep):
        pb_copy(k).wait_recv()
    total = pbs[mr].astype(F32)
    for k in range(1, n_rep):
        total = total + pbr[k].astype(F32)
    pbr[0] = total.astype(BF)
    for j in range(rows):
        dh = gout[block(j)].astype(F32) + dot(lval[block(j)], pbr[0, block(j)], ((0,), (0,)))
        spread_types(j, dh * slope_silu(z1s[block(j)]))

    rs_begin(0)
    for s in range(depth):
        rs_step(1, s)
        rs_step(0, s)
    for s in reversed(range(depth)):
        gat_step(1, s)
        gat_step(0, s)

    for layer in range(2):
        loop_picks(layer, lambda copy: copy.wait_send())
        for k in range(1, n_rep):
            ag_copy(layer, k).wait_send()
        for q in range(streams):
            for s in range(depth):
                rs_copy(layer, q, s).wait_send()
                gat_copy(layer, q, s).wait_send()
    for k in range(1, n_rep):
        pb_copy(k).wait_send()


def shards(
    n_dom, n_rep,
    feats, hist_one, local_val, halo_val, halo_send, halo_tile, tile_type, w_one, w_two, grad_out,
):
    nodes, cols = feats.shape
    tile = local_val.shape[1]
    width, experts, _ = w_one.shape
    cap = halo_send.shape[2]
    pad = max(cap, 16)
    picks = jnp.pad(halo_send[0], ((0, 0), (0, pad - cap))).reshape(n_dom * pad, 1)
    types = tile_type[0]
    chosen_one = jnp.take(w_one, types, axis=1, mode="clip").transpose(1, 0, 2)
    chosen_two = jnp.take(w_two, types, axis=1, mode="clip").transpose(1, 0, 2)

    def per_row(table):
        return jnp.repeat(table[0], tile).reshape(nodes, 1)

    orders = bit_orders(n_dom)
    streams, depth = len(orders), len(orders[0])
    length = experts * width // streams
    vmem = pl.BlockSpec(memory_space=pltpu.VMEM)
    dma = pltpu.SemaphoreType.DMA
    summed = jax.ShapeDtypeStruct((streams, length, cols), BF)
    h_two, h_one, g_one, g_two = pl.pallas_call(
        functools.partial(step_kernel, n_dom, n_rep, cap, tile),
        out_shape=(
            jax.ShapeDtypeStruct((nodes, cols), BF),
            jax.ShapeDtypeStruct((nodes, cols), BF),
            summed,
            summed,
        ),
        in_specs=[vmem] * 10,
        out_specs=(vmem,) * 4,
        scratch_shapes=[
            pltpu.VMEM((2, n_dom * pad, cols), BF),
            pltpu.VMEM((2, n_dom * pad, cols), BF),
            pltpu.VMEM((nodes, width), BF),
            pltpu.VMEM((nodes, width), BF),
            pltpu.VMEM((n_rep, nodes, cols), BF),
            pltpu.VMEM((n_rep, nodes, cols), BF),
            pltpu.VMEM((nodes, cols), F32),
            pltpu.VMEM((nodes, experts * cols), BF),
            pltpu.VMEM((nodes, n_dom * cap), BF),
            pltpu.VMEM((2, streams, length, cols), F32),
            pltpu.VMEM((2, streams, length, cols), BF),
            pltpu.VMEM((2, streams, length, cols), BF),
            dma((2, n_dom)),
            dma((2, n_dom)),
            dma((2, n_rep)),
            dma((2, n_rep)),
            dma((n_rep,)),
            dma((n_rep,)),
            dma((2, streams, depth)),
            dma((2, streams, depth)),
            dma((2, streams, depth)),
            dma((2, streams, depth)),
        ],
        compiler_params=pltpu.CompilerParams(
            collective_id=0, has_side_effects=True, vmem_limit_bytes=40 * 1024 * 1024
        ),
    )(
        feats, hist_one, local_val, halo_val, picks, per_row(halo_tile), per_row(tile_type),
        chosen_one, chosen_two, grad_out,
    )

    def spread(grad):
        parts = grad.reshape(streams, experts, width // streams, cols)
        return parts.transpose(0, 2, 1, 3).reshape(width, experts, cols).astype(F32)

    return h_two, h_one, spread(g_one), spread(g_two)


def solution(mesh):
    in_specs = (
        P("dom", "rep"),
        P("dom", "rep"),
        P("dom", None),
        P("dom", None),
        P("dom", None, None),
        P("dom", None),
        P("dom", None),
        P(None, None, "rep"),
        P(None, None, "rep"),
        P("dom", "rep"),
    )
    out_specs = (P("dom", "rep"), P("dom", "rep"), P(None, None, "rep"), P(None, None, "rep"))
    body = functools.partial(shards, mesh.shape["dom"], mesh.shape["rep"])
    return jax.shard_map(body, mesh=mesh, in_specs=in_specs, out_specs=out_specs, check_vma=False)
```

time: 269 us -> 104 us (0.39)
  waiting for transfers between devices: 178 us -> 0 us
  Pallas kernels: 0 us -> 86.4 us
  blocking collectives: 29.4 us -> 0 us
  between operations: 14.4 us -> 0.8 us
  starting transfers between devices: 13.5 us -> 0 us
  matrix products: 9.75 us -> 0 us
  local copies, waits for them, and re-layouts: 20.4 us -> 15.5 us
  other arithmetic: 3.85 us -> 1.05 us
    psum x1 -> x0, waiting for transfers between devices: 158 us -> none  [shards(): lax.psum((grad_term(agg_one, dz_one, onehot), grad_term(agg_two, dz_two,...]
    pallas_call x0 -> x1, Pallas kernels: none -> 86.4 us  [shards(): pl.pallas_call(functools.partial(step_kernel, n_dom, n_rep, cap, tile), o...]
    all_gather x4 -> x0, blocking collectives: 29.4 us -> none  [the longest x2 15 us: mix_layer(): lax.all_gather(source, 'rep', axis=1, tiled=True)]
    unnamed x3 -> x0, waiting for transfers between devices: 19.1 us -> none
    all_to_all x2 -> x0, starting transfers between devices: 13.4 us -> none  [pull_rows(): lax.all_to_all(picked, 'dom', split_axis=0, concat_axis=0, tiled=True)]
    dot_general x11 -> x0, matrix products: 9.75 us -> none  [the longest x2 3.8 us: grad_term(): return jnp.einsum('je,jdc->dec', onehot, per_tile)]
    unnamed x37 -> x14, local copies, waits for them, and re-layouts: 8.27 us -> 1.35 us
    gather x6 -> x4, local copies, waits for them, and re-layouts: 12 us -> 6.33 us  [the longest x2 3.33 us: shards(): chosen_one = jnp.take(w_one, types, axis=1, mode='clip').transpose(1, 0, 2)]
  transfers between devices with their start and end apart: 4 -> 0, of which waited for: 3 -> 0; matrix products, arithmetic and copies ran while one was open for 4% -> 0% of each run, Pallas kernels for 0% -> 0%
where the time goes in v1:
time: 104 us
  Pallas kernels  86.4 us (83%)
  local copies, waits for them, and re-layouts  15.5 us (15%)
  other arithmetic  1.05 us (1%)
    pallas_call x1, Pallas kernels, shards(): pl.pallas_call(functools.partial(step_kernel, n_dom, n_rep, cap, tile), o...  86.4 us
    convert_element_type x2, local copies, waits for them, and re-layouts, spread(): return parts.transpose(0, 2, 1, 3).reshape(width, experts, cols).astype(F32)  5.07 us
    gather x2, local copies, waits for them, and re-layouts, shards(): chosen_one = jnp.take(w_one, types, axis=1, mode='clip').transpose(1, 0, 2)  3.33 us
    gather x2, local copies, waits for them, and re-layouts, shards(): chosen_two = jnp.take(w_two, types, axis=1, mode='clip').transpose(1, 0, 2)  3 us

profile of v1, /device:TPU:0, one launch (start us, length us, event | category | flops | bytes accessed | tf_op | source)
XLA Modules:
  0.0 103.7 jit_solution(15742360560005790413)
XLA Ops:
  0.6 0.0 copy-start
  0.6 0.8 broadcast_in_dim.11
  1.5 0.7 broadcast_in_dim.12
  2.2 0.7 pad_clamp_fusion
  2.8 0.1 copy.18.types
  3.0 0.1 copy.17.htile
  3.2 0.9 reshape.48.picks
  4.0 0.0 copy-done
  4.1 2.9 %gather_fusion.1 = bf16[4,512,128]{2,0,1:T(4,128)(2,1)S(1)} fusion(bf16[512,8,128]{2,1,0:T(8,128)(2,1)S(1)} %copy-done, s32[1024]{0:T(1024)S(1)} %pad_clamp_fusion), kind=kCustom, calls=%fused_computation.1 | custom fusion | bytes 1048592 | tf_op jit(solution)/shard_map/jit(_take)/gather | solution.py:296
  7.0 0.1 copy.20.w2
  7.1 0.0 copy-start.1
  7.1 0.0 copy-start.2
  7.1 0.0 copy-start.3
  7.1 0.0 copy-start.4
  7.1 0.0 copy-start.5
  7.1 3.3 %gather_fusion = bf16[4,512,128]{2,0,1:T(4,128)(2,1)S(1)} fusion(bf16[512,8,128]{2,1,0:T(8,128)(2,1)} %param.17, s32[1024]{0:T(1024)S(1)} %pad_clamp_fusion), kind=kCustom, calls=%fused_computation | custom fusion | bytes 1048592 | tf_op jit(solution)/shard_map/jit(_take)/gather | solution.py:295
  10.4 0.1 copy.19.w1
  10.5 0.0 copy-done.1
  10.5 0.0 copy-done.2
  10.5 0.0 copy-done.3
  10.5 0.0 copy-done.4
  10.5 0.0 copy-done.5
  10.5 86.4 %shard_map.129 = (bf16[512,128]{1,0:T(8,128)(2,1)S(1)}, bf16[512,128]{1,0:T(8,128)(2,1)S(1)}, bf16[2,2048,128]{2,1,0:T(8,128)(2,1)S(1)}, bf16[2,2048,128]{2,1,0:T(8,128)(2,1)S(1)}) custom-call(bf16[512,128]{1,0:T(8,128)(2,1)S(1)} %copy-done.1, bf16[512,128]{1,0:T(8,128)(2,1)S(1)} %copy-done.2, bf16[512,128]{1,0:T(8,128)(2,1)S(1)} %copy-done.3, ...), custom_call_target="tpu_custom_call" | custom-call | tf_op jit(solution)/shard_map/pallas_call | solution.py:307
  96.9 0.2 convert_bitcast_fusion.1
  97.1 2.5 %copy.21 = f32[2,256,8,128]{3,2,1,0:T(8,128)} copy(f32[2,256,8,128]{3,1,2,0:T(8,128)S(1)} %convert_bitcast_fusion.1) | data formatting | bytes 4194304 | tf_op jit(solution)/shard_map/convert_element_type | solution.py:351
  99.7 0.2 convert_bitcast_fusion
  99.9 2.5 %copy.22 = f32[2,256,8,128]{3,2,1,0:T(8,128)} copy(f32[2,256,8,128]{3,1,2,0:T(8,128)S(1)} %convert_bitcast_fusion) | data formatting | bytes 4194304 | tf_op jit(solution)/shard_map/convert_element_type | solution.py:351
  102.4 0.7 copy.25
  103.1 0.7 copy.26
Async XLA Ops:
  0.6 3.4 %copy-start = (bf16[512,8,128]{2,1,0:T(8,128)(2,1)S(1)}, bf16[512,8,128]{2,1,0:T(8,128)(2,1)}, u32[]{:S(2)}) copy-start(bf16[512,8,128]{2,1,0:T(8,128)(2,1)} %param.18) | copy-start | bytes 3145732
  7.1 3.4 %copy-start.1 = (bf16[512,128]{1,0:T(8,128)(2,1)S(1)}, bf16[512,128]{1,0:T(8,128)(2,1)}, u32[]{:S(2)}) copy-start(bf16[512,128]{1,0:T(8,128)(2,1)} %feats.1) | copy-start | bytes 393220
  7.1 3.4 %copy-start.2 = (bf16[512,128]{1,0:T(8,128)(2,1)S(1)}, bf16[512,128]{1,0:T(8,128)(2,1)}, u32[]{:S(2)}) copy-start(bf16[512,128]{1,0:T(8,128)(2,1)} %hist.1) | copy-start | bytes 393220
  7.1 3.4 %copy-start.3 = (bf16[512,128]{1,0:T(8,128)(2,1)S(1)}, bf16[512,128]{1,0:T(8,128)(2,1)}, u32[]{:S(2)}) copy-start(bf16[512,128]{1,0:T(8,128)(2,1)} %lval.1) | copy-start | bytes 393220
  7.1 3.4 %copy-start.4 = (bf16[512,128]{1,0:T(8,128)(2,1)S(1)}, bf16[512,128]{1,0:T(8,128)(2,1)}, u32[]{:S(2)}) copy-start(bf16[512,128]{1,0:T(8,128)(2,1)} %hval.1) | copy-start | bytes 393220
  7.1 3.4 %copy-start.5 = (bf16[512,128]{1,0:T(8,128)(2,1)S(1)}, bf16[512,128]{1,0:T(8,128)(2,1)}, u32[]{:S(2)}) copy-start(bf16[512,128]{1,0:T(8,128)(2,1)} %gout.1) | copy-start | bytes 393220

commit v2 on v1

--- a/solution.py
+++ b/solution.py
@@ -10,7 +10,6 @@
 MESH = pl.DeviceIdType.MESH
 BF = jnp.bfloat16
 F32 = jnp.float32
-STREAMS = 2
 
 
 def sigmoid(value):
@@ -29,14 +28,14 @@
 def bit_orders(n_dom):
     bits = list(range(n_dom.bit_length() - 1))
     swapped = [bits[1], bits[0]] + bits[2:] if len(bits) > 1 else bits
-    return [bits, swapped][:STREAMS]
+    return [bits, bits, swapped, bits] if n_dom <= 64 else [bits, swapped]
 
 
 def step_kernel(
     n_dom, n_rep, cap, tile,
     feats, hist, lval, hval, picks, htile, types, w1, w2, gout,
-    h2_out, h1_out, res1, res2,
-    picked, halo, agg1, agg2, pbs, pbr, z1s, dzm, spread_halo, acc, sbuf, rbuf,
+    h2_out, h1_out, g1_out, g2_out,
+    picked, halo, agg1, agg2, pbs, pbr, z1s, dzm, spread_halo, acc, sbuf, rbuf, res, wide, wt,
     pick_send, pick_recv, ag_send, ag_recv, pb_send, pb_recv, rs_send, rs_recv, gat_send, gat_recv,
 ):
     nodes, cols = feats.shape
@@ -60,12 +59,16 @@
             barrier, inc=1, device_id={"rep": (mr + k) % n_rep}, device_id_type=MESH
         )
 
-    onehot = (
-        picks[...] == lax.broadcasted_iota(jnp.int32, (n_dom * pad, nodes), 1)
-    ).astype(F32).astype(BF)
-    picked[0] = dot(onehot, feats[...]).astype(BF)
-    picked[1] = dot(onehot, hist[...]).astype(BF)
-    pl.semaphore_wait(barrier, n_dom - 1 + n_rep - 1)
+    node_ids = lax.broadcasted_iota(jnp.int32, (nodes, pad), 0)
+
+    def pick_rows(layer):
+        def body(p, carry):
+            onehot = (picks[pl.ds(p, 1), :] == node_ids).astype(F32).astype(BF)
+            here = pl.ds(pl.multiple_of(p * pad, pad), pad)
+            picked[layer, here] = dot(onehot, (feats, hist)[layer][...], ((0,), (0,))).astype(BF)
+            return carry
+
+        lax.fori_loop(0, n_dom, body, 0, unroll=n_dom <= 8)
 
     def pick_copy(layer, k):
         to = (me + k) % n_dom
@@ -87,6 +90,9 @@
 
     own = pl.ds(pl.multiple_of(me * pad, pad), pad)
     for layer in range(2):
+        pick_rows(layer)
+        if layer == 0:
+            pl.semaphore_wait(barrier, n_dom - 1 + n_rep - 1)
         loop_picks(layer, lambda copy: copy.start())
         halo[layer, own] = picked[layer, own]
 
@@ -105,75 +111,92 @@
     def own_cols(r):
         return pl.ds(pl.multiple_of(r * cols, cols), cols)
 
-    def ag_copy(layer, k):
-        part = (agg1, agg2)[layer].at[:, own_cols(mr)]
+    def ag_copy(layer, j, k):
+        part = (agg1, agg2)[layer].at[block(j), own_cols(mr)]
         return pltpu.make_async_remote_copy(
             src_ref=part,
             dst_ref=part,
-            send_sem=ag_send.at[layer, k],
-            recv_sem=ag_recv.at[layer, k],
+            send_sem=ag_send.at[layer, j, k],
+            recv_sem=ag_recv.at[layer, j, k],
             device_id={"rep": (mr + k) % n_rep},
             device_id_type=MESH,
         )
 
-    def aggregate(layer, source):
+    def pb_copy(j, k):
+        to = (mr + k) % n_rep
+        return pltpu.make_async_remote_copy(
+            src_ref=pbs.at[to, block(j)],
+            dst_ref=pbr.at[k, block(j)],
+            send_sem=pb_send.at[j, k],
+            recv_sem=pb_recv.at[j, k],
+            device_id={"rep": to},
+            device_id_type=MESH,
+        )
+
+    def unpack_weights(layer):
+        wide[...] = (w1, w2)[layer][...].astype(F32).reshape(width * experts, cols)
+        for t in range(experts):
+            wt[layer, :, t * cols : (t + 1) * cols] = wide[
+                pl.ds(t, width, stride=experts)
+            ].astype(BF)
+
+    def is_type(j, t):
+        return (types[:, j : j + 1] == t).astype(F32)
+
+    def aggregate(layer, j, local):
         full = (agg1, agg2)[layer]
-        local = [dot(lval[block(j)], source[block(j)]) for j in range(rows)]
-        loop_picks(layer, lambda copy: copy.wait_recv())
-        compact(layer)
-        for j in range(rows):
-            there = dot(spread_halo[block(j)], halo[layer, pl.ds(0, n_dom * cap)])
-            full[block(j), own_cols(mr)] = (local[j] + there).astype(BF)
-        for k in range(1, n_rep):
-            ag_copy(layer, k).start()
-        for k in range(1, n_rep):
-            ag_copy(layer, k).wait_recv()
-
-    for b in range(n_dom * cap // tile):
-        held = (htile[...] == b).astype(F32)
-        spread_halo[:, b * tile : (b + 1) * tile] = (hval[...].astype(F32) * held).astype(BF)
-
-    aggregate(0, feats)
-    for j in range(rows):
-        z = dot(agg1[block(j)], w1[j])
-        z1s[block(j)] = z
-        h1_out[block(j)] = (feats[block(j)].astype(F32) + z * sigmoid(z)).astype(BF)
-
-    aggregate(1, h1_out)
+        there = dot(spread_halo[block(j)], halo[layer, pl.ds(0, n_dom * cap)])
+        full[block(j), own_cols(mr)] = (local + there).astype(BF)
+        for k in range(1, n_rep):
+            ag_copy(layer, j, k).start()
+
+    def expert(layer, j):
+        for k in range(1, n_rep):
+            ag_copy(layer, j, k).wait_recv()
+        every = dot((agg1, agg2)[layer][block(j)], wt[layer])
+        z = every[:, :cols] * is_type(j, 0)
+        for t in range(1, experts):
+            z = z + every[:, t * cols : (t + 1) * cols] * is_type(j, t)
+        return z
 
     def spread_types(j, dz):
         for t in range(experts):
-            held = (types[block(j)] == t).astype(F32)
-            dzm[block(j), t * cols : (t + 1) * cols] = (dz * held).astype(BF)
-
-    for j in range(rows):
-        z = dot(agg2[block(j)], w2[j])
-        h2_out[block(j)] = (h1_out[block(j)].astype(F32) + z * sigmoid(z)).astype(BF)
-        dz = gout[block(j)].astype(F32) * slope_silu(z)
-        spread_types(j, dz)
-        back = dot(dz.astype(BF), w2[j], ((1,), (1,))).astype(BF)
+            dzm[block(j), t * cols : (t + 1) * cols] = (dz * is_type(j, t)).astype(BF)
+
+    for j in range(rows):
+        own_tile = hval[block(j)].astype(F32)
+        for b in range(n_dom * cap // tile):
+            held = (htile[:, j : j + 1] == b).astype(F32)
+            spread_halo[block(j), b * tile : (b + 1) * tile] = (own_tile * held).astype(BF)
+    unpack_weights(0)
+    local = [dot(lval[block(j)], feats[block(j)]) for j in range(rows)]
+    loop_picks(0, lambda copy: copy.wait_recv())
+    compact(0)
+    for j in range(rows):
+        aggregate(0, j, local[j])
+    unpack_weights(1)
+    loop_picks(1, lambda copy: copy.wait_recv())
+    compact(1)
+    for j in range(rows):
+        z = expert(0, j)
+        h = (feats[block(j)].astype(F32) + z * sigmoid(z)).astype(BF)
+        z1s[block(j)] = z
+        h1_out[block(j)] = h
+        aggregate(1, j, dot(lval[block(j)], h))
+    for j in range(rows):
+        z = expert(1, j)
+        spread_types(j, gout[block(j)].astype(F32) * slope_silu(z))
+        back = dot(dzm[block(j)], wt[1], ((1,), (1,))).astype(BF)
         for r in range(n_rep):
             pbs[r, block(j)] = back[:, r * cols : (r + 1) * cols]
-
-    def pb_copy(k):
-        to = (mr + k) % n_rep
-        return pltpu.make_async_remote_copy(
-            src_ref=pbs.at[to],
-            dst_ref=pbr.at[k],
-            send_sem=pb_send.at[k],
-            recv_sem=pb_recv.at[k],
-            device_id={"rep": to},
-            device_id_type=MESH,
-        )
-
-    for k in range(1, n_rep):
-        pb_copy(k).start()
+        for k in range(1, n_rep):
+            pb_copy(j, k).start()
+        h2_out[block(j)] = (h1_out[block(j)].astype(F32) + z * sigmoid(z)).astype(BF)
 
     orders = bit_orders(n_dom)
     streams = len(orders)
     length = acc.shape[2]
     sub = width // streams
-    results = (res1, res2)
 
     def my_bit(b):
         return (me // (1 << b)) % 2
@@ -204,7 +227,7 @@
 
     def gat_copy(layer, q, s):
         b, size = orders[q][s], length >> (s + 1)
-        part = results[layer].at[q, span(base(q, s + 1), size)]
+        part = res.at[layer, q, span(base(q, s + 1), size)]
         return pltpu.make_async_remote_copy(
             src_ref=part,
             dst_ref=part,
@@ -240,7 +263,7 @@
                 acc[layer, q, kept] += got
                 rs_send_half(layer, q, s + 1)
             else:
-                results[layer][q, kept] = (acc[layer, q, kept] + got).astype(BF)
+                res[layer, q, kept] = (acc[layer, q, kept] + got).astype(BF)
                 gat_copy(layer, q, s).start()
 
     def gat_step(layer, s):
@@ -249,36 +272,49 @@
             if s > 0:
                 gat_copy(layer, q, s - 1).start()
 
+    def write_out(layer):
+        out = (g1_out, g2_out)[layer]
+        for q in range(streams):
+            for t in range(experts):
+                out[pl.ds(q * sub * experts + t, sub, stride=experts)] = res[
+                    layer, q, t * sub : (t + 1) * sub
+                ].astype(F32)
+
     rs_begin(1)
-
-    for k in range(1, n_rep):
-        pb_copy(k).wait_recv()
-    total = pbs[mr].astype(F32)
-    for k in range(1, n_rep):
-        total = total + pbr[k].astype(F32)
-    pbr[0] = total.astype(BF)
-    for j in range(rows):
-        dh = gout[block(j)].astype(F32) + dot(lval[block(j)], pbr[0, block(j)], ((0,), (0,)))
+    for j in range(rows):
+        for k in range(1, n_rep):
+            pb_copy(j, k).wait_recv()
+        total = pbs[mr, block(j)].astype(F32)
+        for k in range(1, n_rep):
+            total = total + pbr[k, block(j)].astype(F32)
+        dh = gout[block(j)].astype(F32) + dot(lval[block(j)], total.astype(BF), ((0,), (0,)))
         spread_types(j, dh * slope_silu(z1s[block(j)]))
 
     rs_begin(0)
-    for s in range(depth):
-        rs_step(1, s)
-        rs_step(0, s)
-    for s in reversed(range(depth)):
-        gat_step(1, s)
-        gat_step(0, s)
+    steps = [(rs_step, s) for s in range(depth)] + [(gat_step, s) for s in reversed(range(depth))]
+    for i in range(2 * depth + 1):
+        if i < 2 * depth:
+            act, s = steps[i]
+            act(1, s)
+        if i > 0:
+            act, s = steps[i - 1]
+            act(0, s)
+        if i == 2 * depth - 1:
+            write_out(1)
+    write_out(0)
 
     for layer in range(2):
         loop_picks(layer, lambda copy: copy.wait_send())
-        for k in range(1, n_rep):
-            ag_copy(layer, k).wait_send()
+        for j in range(rows):
+            for k in range(1, n_rep):
+                ag_copy(layer, j, k).wait_send()
         for q in range(streams):
             for s in range(depth):
                 rs_copy(layer, q, s).wait_send()
                 gat_copy(layer, q, s).wait_send()
-    for k in range(1, n_rep):
-        pb_copy(k).wait_send()
+    for j in range(rows):
+        for k in range(1, n_rep):
+            pb_copy(j, k).wait_send()
 
 
 def shards(
@@ -290,20 +326,16 @@
     width, experts, _ = w_one.shape
     cap = halo_send.shape[2]
     pad = max(cap, 16)
-    picks = jnp.pad(halo_send[0], ((0, 0), (0, pad - cap))).reshape(n_dom * pad, 1)
-    types = tile_type[0]
-    chosen_one = jnp.take(w_one, types, axis=1, mode="clip").transpose(1, 0, 2)
-    chosen_two = jnp.take(w_two, types, axis=1, mode="clip").transpose(1, 0, 2)
-
-    def per_row(table):
-        return jnp.repeat(table[0], tile).reshape(nodes, 1)
-
+    picks = halo_send[0]
+    if pad > cap:
+        picks = jnp.pad(picks, ((0, 0), (0, pad - cap)))
+    rows = nodes // tile
     orders = bit_orders(n_dom)
     streams, depth = len(orders), len(orders[0])
     length = experts * width // streams
     vmem = pl.BlockSpec(memory_space=pltpu.VMEM)
     dma = pltpu.SemaphoreType.DMA
-    summed = jax.ShapeDtypeStruct((streams, length, cols), BF)
+    summed = jax.ShapeDtypeStruct((width * experts, cols), F32)
     h_two, h_one, g_one, g_two = pl.pallas_call(
         functools.partial(step_kernel, n_dom, n_rep, cap, tile),
         out_shape=(
@@ -327,12 +359,15 @@
             pltpu.VMEM((2, streams, length, cols), F32),
             pltpu.VMEM((2, streams, length, cols), BF),
             pltpu.VMEM((2, streams, length, cols), BF),
+            pltpu.VMEM((2, streams, length, cols), BF),
+            pltpu.VMEM((width * experts, cols), F32),
+            pltpu.VMEM((2, width, experts * cols), BF),
             dma((2, n_dom)),
             dma((2, n_dom)),
-            dma((2, n_rep)),
-            dma((2, n_rep)),
-            dma((n_rep,)),
-            dma((n_rep,)),
+            dma((2, rows, n_rep)),
+            dma((2, rows, n_rep)),
+            dma((rows, n_rep)),
+            dma((rows, n_rep)),
             dma((2, streams, depth)),
             dma((2, streams, depth)),
             dma((2, streams, depth)),
@@ -342,15 +377,12 @@
             collective_id=0, has_side_effects=True, vmem_limit_bytes=40 * 1024 * 1024
         ),
     )(
-        feats, hist_one, local_val, halo_val, picks, per_row(halo_tile), per_row(tile_type),
-        chosen_one, chosen_two, grad_out,
+        feats, hist_one, local_val, halo_val, picks, halo_tile, tile_type,
+        w_one, w_two, grad_out,
     )
 
-    def spread(grad):
-        parts = grad.reshape(streams, experts, width // streams, cols)
-        return parts.transpose(0, 2, 1, 3).reshape(width, experts, cols).astype(F32)
-
-    return h_two, h_one, spread(g_one), spread(g_two)
+    shape = (width, experts, cols)
+    return h_two, h_one, g_one.reshape(shape), g_two.reshape(shape)
 
 
 def solution(mesh):

time: 104 us -> 97.1 us (0.934)
  Pallas kernels: 86.4 us -> 83.2 us
  local copies, waits for them, and re-layouts: 15.5 us -> 12.9 us
  other arithmetic: 1.05 us -> 0 us
    unnamed x14 -> x24, local copies, waits for them, and re-layouts: 1.35 us -> 12.9 us
    gather x4 -> x0, local copies, waits for them, and re-layouts: 6.33 us -> none  [the longest x2 3.33 us: shards(): chosen_one = jnp.take(w_one, types, axis=1, mode='clip').transpose(1, 0, 2)]
    convert_element_type x2 -> x0, local copies, waits for them, and re-layouts: 5.07 us -> none  [spread(): return parts.transpose(0, 2, 1, 3).reshape(width, experts, cols).astype(F32)]
    pallas_call x1, Pallas kernels: 86.4 us -> 83.2 us  [shards(): pl.pallas_call(functools.partial(step_kernel, n_dom, n_rep, cap, tile), o...]
    broadcast_in_dim x2 -> x0, local copies, waits for them, and re-layouts: 1.54 us -> none  [per_row(): return jnp.repeat(table[0], tile).reshape(nodes, 1)]
where the time goes in v2:
time: 97.1 us; the launch traced here: 96.8 us
  Pallas kernels  83.2 us (86%)
  local copies, waits for them, and re-layouts  12.9 us (13%)
    pallas_call x1, Pallas kernels, shards(): pl.pallas_call(functools.partial(step_kernel, n_dom, n_rep, cap, tile), o...  83.2 us
    unnamed x24, local copies, waits for them, and re-layouts  12.9 us

profile of v2, /device:TPU:0, one launch (start us, length us, event | category | flops | bytes accessed | tf_op | source)
XLA Modules:
  0.0 96.8 jit_solution(4552326570065217996)
XLA Ops:
  0.6 0.0 copy-start
  0.6 1.2 %copy-done = bf16[512,8,128]{2,1,0:T(8,128)(2,1)S(1)} copy-done((bf16[512,8,128]{2,1,0:T(8,128)(2,1)S(1)}, bf16[512,8,128]{2,1,0:T(8,128)(2,1)}, u32[]{:S(2)}) %copy-start) | copy-done | bytes 1048600
  1.9 0.0 copy-start.1
  1.9 1.2 %copy-done.1 = bf16[512,8,128]{2,1,0:T(8,128)(2,1)S(1)} copy-done((bf16[512,8,128]{2,1,0:T(8,128)(2,1)S(1)}, bf16[512,8,128]{2,1,0:T(8,128)(2,1)}, u32[]{:S(2)}) %copy-start.1) | copy-done | bytes 1048600
  3.1 0.0 copy-start.2
  3.1 0.9 copy-done.2
  4.0 0.0 copy-start.3
  4.0 0.9 copy-done.3
  4.9 0.0 copy-start.4
  4.9 0.9 copy-done.4
  5.8 0.0 copy-start.5
  5.8 0.9 copy-done.5
  6.7 0.0 copy-start.6
  6.7 0.9 copy-done.6
  7.6 0.0 copy-start.7
  7.6 0.7 copy-done.7
  8.3 0.0 copy-start.8
  8.3 0.7 copy-done.8
  9.0 0.0 copy-start.9
  9.0 0.7 copy-done.9
  9.6 83.2 %shard_map.129 = (bf16[512,128]{1,0:T(8,128)(2,1)S(1)}, bf16[512,128]{1,0:T(8,128)(2,1)S(1)}, f32[4096,128]{1,0:T(8,128)S(1)}, f32[4096,128]{1,0:T(8,128)S(1)}) custom-call(bf16[512,128]{1,0:T(8,128)(2,1)S(1)} %copy-done.2, bf16[512,128]{1,0:T(8,128)(2,1)S(1)} %copy-done.3, bf16[512,128]{1,0:T(8,128)(2,1)S(1)} %copy-done.4, bf16[512,128]{1,0:T(8,128)(2,1)S(1)} %copy-done.5, ...), custom_call_target="tpu_custom_call" | custom-call | tf_op jit(solution)/shard_map/pallas_call | solution.py:339
  92.8 0.7 copy.18
  93.5 0.7 copy.19
  94.1 1.3 %copy.20 = f32[512,8,128]{2,1,0:T(8,128)} copy(f32[512,8,128]{2,1,0:T(8,128)S(1)} %bitcast.4) | data formatting | bytes 4194304
  95.4 1.3 %copy.21 = f32[512,8,128]{2,1,0:T(8,128)} copy(f32[512,8,128]{2,1,0:T(8,128)S(1)} %bitcast.3) | data formatting | bytes 4194304
Async XLA Ops:
  0.6 1.2 %copy-start = (bf16[512,8,128]{2,1,0:T(8,128)(2,1)S(1)}, bf16[512,8,128]{2,1,0:T(8,128)(2,1)}, u32[]{:S(2)}) copy-start(bf16[512,8,128]{2,1,0:T(8,128)(2,1)} %w1.1) | copy-start | bytes 3145732
  1.9 1.2 %copy-start.1 = (bf16[512,8,128]{2,1,0:T(8,128)(2,1)S(1)}, bf16[512,8,128]{2,1,0:T(8,128)(2,1)}, u32[]{:S(2)}) copy-start(bf16[512,8,128]{2,1,0:T(8,128)(2,1)} %w2.1) | copy-start | bytes 3145732
  3.1 0.9 copy-start.2
  4.0 0.9 copy-start.3
  4.9 0.9 copy-start.4
  5.8 0.9 copy-start.5
  6.7 0.9 copy-start.6
  7.6 0.7 copy-start.7
  8.3 0.7 copy-start.8
  9.0 0.7 copy-start.9

commit v3 on v2

--- a/solution.py
+++ b/solution.py
@@ -10,6 +10,7 @@
 MESH = pl.DeviceIdType.MESH
 BF = jnp.bfloat16
 F32 = jnp.float32
+VMEM_LIMIT = 62 * 1024 * 1024
 
 
 def sigmoid(value):
@@ -33,9 +34,11 @@
 
 def step_kernel(
     n_dom, n_rep, cap, tile,
-    feats, hist, lval, hval, picks, htile, types, w1, w2, gout,
-    h2_out, h1_out, g1_out, g2_out,
-    picked, halo, agg1, agg2, pbs, pbr, z1s, dzm, spread_halo, acc, sbuf, rbuf, res, wide, wt,
+    feats_in, hist_in, lval_in, hval_in, picks_in, htile_in, types_in, w1_in, w2_in, gout_in,
+    h2_hbm, h1_hbm, g1_hbm, g2_hbm,
+    h2_out, h1_out, g1_out, g2_out, out_sem, grad_sem,
+    picked, halo, agg1, agg2, pbs, pbr, z1s, dzm, spread_halo, acc, sbuf, rbuf, res, wide, chosen,
+    feats, hist, lval, hval, picks, htile, types, w1, w2, gout, onehot, in_sem,
     pick_send, pick_recv, ag_send, ag_recv, pb_send, pb_recv, rs_send, rs_recv, gat_send, gat_recv,
 ):
     nodes, cols = feats.shape
@@ -43,6 +46,19 @@
     width = agg1.shape[1]
     experts = dzm.shape[1] // cols
     pad = picked.shape[1] // n_dom
+    outer = (feats_in, hist_in, lval_in, hval_in, picks_in, htile_in, types_in, w1_in, w2_in, gout_in)
+    inner = (feats, hist, lval, hval, picks, htile, types, w1, w2, gout)
+    loads = {
+        id(held): pltpu.make_async_copy(given, held, in_sem.at[n])
+        for n, (given, held) in enumerate(zip(outer, inner))
+    }
+    for held in (picks, feats, hist, w1, lval, htile, types, hval, w2, gout):
+        loads[id(held)].start()
+
+    def ready(*refs):
+        for held in refs:
+            loads[id(held)].wait()
+
     me = lax.axis_index("dom")
     mr = lax.axis_index("rep")
     barrier = pltpu.get_barrier_semaphore()
@@ -61,14 +77,13 @@
 
     node_ids = lax.broadcasted_iota(jnp.int32, (nodes, pad), 0)
 
-    def pick_rows(layer):
-        def body(p, carry):
-            onehot = (picks[pl.ds(p, 1), :] == node_ids).astype(F32).astype(BF)
-            here = pl.ds(pl.multiple_of(p * pad, pad), pad)
-            picked[layer, here] = dot(onehot, (feats, hist)[layer][...], ((0,), (0,))).astype(BF)
-            return carry
-
-        lax.fori_loop(0, n_dom, body, 0, unroll=n_dom <= 8)
+    ready(picks, feats, hist)
+    for p in range(n_dom):
+        onehot[:, p * pad : (p + 1) * pad] = (picks[p : p + 1, :] == node_ids).astype(F32).astype(BF)
+    both = dot(onehot[...], jnp.concatenate([feats[...], hist[...]], axis=1), ((0,), (0,)))
+    picked[0] = both[:, :cols].astype(BF)
+    picked[1] = both[:, cols:].astype(BF)
+    pl.semaphore_wait(barrier, n_dom - 1 + n_rep - 1)
 
     def pick_copy(layer, k):
         to = (me + k) % n_dom
@@ -90,9 +105,6 @@
 
     own = pl.ds(pl.multiple_of(me * pad, pad), pad)
     for layer in range(2):
-        pick_rows(layer)
-        if layer == 0:
-            pl.semaphore_wait(barrier, n_dom - 1 + n_rep - 1)
         loop_picks(layer, lambda copy: copy.start())
         halo[layer, own] = picked[layer, own]
 
@@ -133,15 +145,27 @@
             device_id_type=MESH,
         )
 
+    def is_type(j, t):
+        return (types[:, j : j + 1] == t).astype(F32)
+
     def unpack_weights(layer):
         wide[...] = (w1, w2)[layer][...].astype(F32).reshape(width * experts, cols)
-        for t in range(experts):
-            wt[layer, :, t * cols : (t + 1) * cols] = wide[
-                pl.ds(t, width, stride=experts)
-            ].astype(BF)
-
-    def is_type(j, t):
-        return (types[:, j : j + 1] == t).astype(F32)
+        held = [[is_type(j, t) for t in range(experts)] for j in range(rows)]
+        chunk = 64
+
+        def body(d, carry):
+            start = pl.multiple_of(d * chunk, chunk)
+            totals = [None] * rows
+            for t in range(experts):
+                part = wide[pl.ds(start * experts + t, chunk, stride=experts)]
+                for j in range(rows):
+                    term = part * held[j][t]
+                    totals[j] = term if t == 0 else totals[j] + term
+            for j in range(rows):
+                chosen[layer, j, pl.ds(start, chunk)] = totals[j].astype(BF)
+            return carry
+
+        lax.fori_loop(0, width // chunk, body, 0)
 
     def aggregate(layer, j, local):
         full = (agg1, agg2)[layer]
@@ -153,16 +177,13 @@
     def expert(layer, j):
         for k in range(1, n_rep):
             ag_copy(layer, j, k).wait_recv()
-        every = dot((agg1, agg2)[layer][block(j)], wt[layer])
-        z = every[:, :cols] * is_type(j, 0)
-        for t in range(1, experts):
-            z = z + every[:, t * cols : (t + 1) * cols] * is_type(j, t)
-        return z
+        return dot((agg1, agg2)[layer][block(j)], chosen[layer, j])
 
     def spread_types(j, dz):
         for t in range(experts):
             dzm[block(j), t * cols : (t + 1) * cols] = (dz * is_type(j, t)).astype(BF)
 
+    ready(lval, hval, htile, types, w1)
     for j in range(rows):
         own_tile = hval[block(j)].astype(F32)
         for b in range(n_dom * cap // tile):
@@ -174,7 +195,9 @@
     compact(0)
     for j in range(rows):
         aggregate(0, j, local[j])
+    ready(w2)
     unpack_weights(1)
+    ready(gout)
     loop_picks(1, lambda copy: copy.wait_recv())
     compact(1)
     for j in range(rows):
@@ -185,12 +208,13 @@
         aggregate(1, j, dot(lval[block(j)], h))
     for j in range(rows):
         z = expert(1, j)
-        spread_types(j, gout[block(j)].astype(F32) * slope_silu(z))
-        back = dot(dzm[block(j)], wt[1], ((1,), (1,))).astype(BF)
+        dz = gout[block(j)].astype(F32) * slope_silu(z)
+        back = dot(dz.astype(BF), chosen[1, j], ((1,), (1,))).astype(BF)
         for r in range(n_rep):
             pbs[r, block(j)] = back[:, r * cols : (r + 1) * cols]
         for k in range(1, n_rep):
             pb_copy(j, k).start()
+        spread_types(j, dz)
         h2_out[block(j)] = (h1_out[block(j)].astype(F32) + z * sigmoid(z)).astype(BF)
 
     orders = bit_orders(n_dom)
@@ -245,10 +269,12 @@
 
     def rs_begin(layer):
         agg = (agg1, agg2)[layer]
+        grad = dot(agg[...], dzm[...], ((0,), (0,)))
         for q in range(streams):
-            grad = dot(agg[:, q * sub : (q + 1) * sub], dzm[...], ((0,), (0,)))
             for t in range(experts):
-                acc[layer, q, t * sub : (t + 1) * sub] = grad[:, t * cols : (t + 1) * cols]
+                acc[layer, q, t * sub : (t + 1) * sub] = grad[
+                    q * sub : (q + 1) * sub, t * cols : (t + 1) * cols
+                ]
             rs_send_half(layer, q, 0)
 
     depth = len(orders[0])
@@ -266,20 +292,36 @@
                 res[layer, q, kept] = (acc[layer, q, kept] + got).astype(BF)
                 gat_copy(layer, q, s).start()
 
+    def grad_write(layer, q):
+        here = pl.ds(q * sub * experts, sub * experts)
+        return pltpu.make_async_copy(
+            (g1_out, g2_out)[layer].at[here],
+            (g1_hbm, g2_hbm)[layer].at[here],
+            grad_sem.at[layer, q],
+        )
+
+    def write_out(layer, q):
+        out = (g1_out, g2_out)[layer]
+        for t in range(experts):
+            out[pl.ds(q * sub * experts + t, sub, stride=experts)] = res[
+                layer, q, t * sub : (t + 1) * sub
+            ].astype(F32)
+        grad_write(layer, q).start()
+
     def gat_step(layer, s):
         for q in range(streams):
             gat_copy(layer, q, s).wait_recv()
             if s > 0:
                 gat_copy(layer, q, s - 1).start()
-
-    def write_out(layer):
-        out = (g1_out, g2_out)[layer]
-        for q in range(streams):
-            for t in range(experts):
-                out[pl.ds(q * sub * experts + t, sub, stride=experts)] = res[
-                    layer, q, t * sub : (t + 1) * sub
-                ].astype(F32)
-
+            else:
+                write_out(layer, q)
+
+    writes = (
+        pltpu.make_async_copy(h1_out, h1_hbm, out_sem.at[0]),
+        pltpu.make_async_copy(h2_out, h2_hbm, out_sem.at[1]),
+    )
+    for copy in writes:
+        copy.start()
     rs_begin(1)
     for j in range(rows):
         for k in range(1, n_rep):
@@ -299,9 +341,6 @@
         if i > 0:
             act, s = steps[i - 1]
             act(0, s)
-        if i == 2 * depth - 1:
-            write_out(1)
-    write_out(0)
 
     for layer in range(2):
         loop_picks(layer, lambda copy: copy.wait_send())
@@ -312,9 +351,21 @@
             for s in range(depth):
                 rs_copy(layer, q, s).wait_send()
                 gat_copy(layer, q, s).wait_send()
+            grad_write(layer, q).wait()
+    for copy in writes:
+        copy.wait()
     for j in range(rows):
         for k in range(1, n_rep):
             pb_copy(j, k).wait_send()
+
+
+def write_back(h2, h1, g1, g2, h2_out, h1_out, g1_out, g2_out, sem):
+    pairs = ((g1, g1_out), (g2, g2_out), (h1, h1_out), (h2, h2_out))
+    copies = [pltpu.make_async_copy(a, b, sem.at[n]) for n, (a, b) in enumerate(pairs)]
+    for copy in copies:
+        copy.start()
+    for copy in copies:
+        copy.wait()
 
 
 def shards(
@@ -330,10 +381,13 @@
     if pad > cap:
         picks = jnp.pad(picks, ((0, 0), (0, pad - cap)))
     rows = nodes // tile
+    operands = (
+        feats, hist_one, local_val, halo_val, picks, halo_tile, tile_type, w_one, w_two, grad_out
+    )
     orders = bit_orders(n_dom)
     streams, depth = len(orders), len(orders[0])
     length = experts * width // streams
-    vmem = pl.BlockSpec(memory_space=pltpu.VMEM)
+    hbm = pl.BlockSpec(memory_space=pltpu.HBM)
     dma = pltpu.SemaphoreType.DMA
     summed = jax.ShapeDtypeStruct((width * experts, cols), F32)
     h_two, h_one, g_one, g_two = pl.pallas_call(
@@ -344,9 +398,15 @@
             summed,
             summed,
         ),
-        in_specs=[vmem] * 10,
-        out_specs=(vmem,) * 4,
+        in_specs=[hbm] * 10,
+        out_specs=(hbm,) * 4,
         scratch_shapes=[
+            pltpu.VMEM((nodes, cols), BF),
+            pltpu.VMEM((nodes, cols), BF),
+            pltpu.VMEM((width * experts, cols), F32),
+            pltpu.VMEM((width * experts, cols), F32),
+            dma((2,)),
+            dma((2, streams)),
             pltpu.VMEM((2, n_dom * pad, cols), BF),
             pltpu.VMEM((2, n_dom * pad, cols), BF),
             pltpu.VMEM((nodes, width), BF),
@@ -361,7 +421,10 @@
             pltpu.VMEM((2, streams, length, cols), BF),
             pltpu.VMEM((2, streams, length, cols), BF),
             pltpu.VMEM((width * experts, cols), F32),
-            pltpu.VMEM((2, width, experts * cols), BF),
+            pltpu.VMEM((2, rows, width, cols), BF),
+            *[pltpu.VMEM(a.shape, a.dtype) for a in operands],
+            pltpu.VMEM((nodes, n_dom * pad), BF),
+            dma((len(operands),)),
             dma((2, n_dom)),
             dma((2, n_dom)),
             dma((2, rows, n_rep)),
@@ -374,12 +437,17 @@
             dma((2, streams, depth)),
         ],
         compiler_params=pltpu.CompilerParams(
-            collective_id=0, has_side_effects=True, vmem_limit_bytes=40 * 1024 * 1024
+            collective_id=0, has_side_effects=True, vmem_limit_bytes=VMEM_LIMIT
         ),
-    )(
-        feats, hist_one, local_val, halo_val, picks, halo_tile, tile_type,
-        w_one, w_two, grad_out,
-    )
+    )(*operands)
+    h_two, h_one, g_one, g_two = pl.pallas_call(
+        write_back,
+        out_shape=tuple(jax.ShapeDtypeStruct(a.shape, a.dtype) for a in (h_two, h_one, g_one, g_two)),
+        in_specs=[pl.BlockSpec(memory_space=pl.ANY)] * 4,
+        out_specs=(hbm,) * 4,
+        scratch_shapes=[dma((4,))],
+        compiler_params=pltpu.CompilerParams(vmem_limit_bytes=VMEM_LIMIT),
+    )(h_two, h_one, g_one, g_two)
 
     shape = (width, experts, cols)
     return h_two, h_one, g_one.reshape(shape), g_two.reshape(shape)

time: 97.1 us -> 220 us (2.27)
  Pallas kernels: 83.2 us -> 220 us
  local copies, waits for them, and re-layouts: 12.9 us -> 0 us
    pallas_call x0 -> x1, Pallas kernels: none -> 136 us  [shards(): pl.pallas_call(write_back, out_shape=tuple((jax.ShapeDtypeStruct(a.shape,...]
    unnamed x24 -> x0, local copies, waits for them, and re-layouts: 12.9 us -> none
where the time goes in v3:
time: 220 us
  Pallas kernels  220 us (100%)
    pallas_call x1, Pallas kernels, shards(): pl.pallas_call(write_back, out_shape=tuple((jax.ShapeDtypeStruct(a.shape,...  136 us
    pallas_call x1, Pallas kernels, shards(): pl.pallas_call(functools.partial(step_kernel, n_dom, n_rep, cap, tile), o...  83.4 us

profile of v3, /device:TPU:0, one launch (start us, length us, event | category | flops | bytes accessed | tf_op | source)
XLA Modules:
  0.0 220.2 jit_solution(5743217608813629539)
XLA Ops:
  0.6 83.4 %shard_map.129 = (bf16[512,128]{1,0:T(8,128)(2,1)}, bf16[512,128]{1,0:T(8,128)(2,1)}, f32[4096,128]{1,0:T(8,128)}, f32[4096,128]{1,0:T(8,128)}) custom-call(bf16[512,128]{1,0:T(8,128)(2,1)} %feats_in.1, bf16[512,128]{1,0:T(8,128)(2,1)} %hist_in.1, bf16[512,128]{1,0:T(8,128)(2,1)} %lval_in.1, bf16[512,128]{1,0:T(8,128)(2,1)} %hval_in.1, s32[8,64]{1,0:T(8,128)} %bitcast.3, ...), custom_call_target="tpu_custom_call" | custom-call | tf_op jit(solution)/shard_map/pallas_call | solution.py:393
  84.1 136.1 %shard_map.130 = (bf16[512,128]{1,0:T(8,128)(2,1)}, bf16[512,128]{1,0:T(8,128)(2,1)}, f32[4096,128]{1,0:T(8,128)}, f32[4096,128]{1,0:T(8,128)}) custom-call(bf16[512,128]{1,0:T(8,128)(2,1)} %get-tuple-element.12.h2, bf16[512,128]{1,0:T(8,128)(2,1)} %get-tuple-element.13.h1, f32[4096,128]{1,0:T(8,128)} %get-tuple-element.14.g1, f32[4096,128]{1,0:T(8,128)} %get-tuple-element.15.g2), custom_call_target="tpu_custom_call" | custom-call | tf_op jit(solution)/shard_map/pallas_call | solution.py:443

commit v4 on v3

--- a/solution.py
+++ b/solution.py
@@ -37,7 +37,7 @@
     feats_in, hist_in, lval_in, hval_in, picks_in, htile_in, types_in, w1_in, w2_in, gout_in,
     h2_hbm, h1_hbm, g1_hbm, g2_hbm,
     h2_out, h1_out, g1_out, g2_out, out_sem, grad_sem,
-    picked, halo, agg1, agg2, pbs, pbr, z1s, dzm, spread_halo, acc, sbuf, rbuf, res, wide, chosen,
+    picked, halo, agg1, agg2, pbs, pbr, pair, z1s, dzm, spread_halo, acc, sbuf, rbuf, res, wide, chosen,
     feats, hist, lval, hval, picks, htile, types, w1, w2, gout, onehot, in_sem,
     pick_send, pick_recv, ag_send, ag_recv, pb_send, pb_recv, rs_send, rs_recv, gat_send, gat_recv,
 ):
@@ -123,27 +123,45 @@
     def own_cols(r):
         return pl.ds(pl.multiple_of(r * cols, cols), cols)
 
+    near = mr + 1 - 2 * (mr % 2)
+    far = (mr + n_rep // 2) % n_rep
+    near_far = (near + n_rep // 2) % n_rep
+
     def ag_copy(layer, j, k):
-        part = (agg1, agg2)[layer].at[block(j), own_cols(mr)]
+        held, to = ((mr, near), (mr, far), (far, near))[k]
+        part = (agg1, agg2)[layer].at[block(j), own_cols(held)]
         return pltpu.make_async_remote_copy(
             src_ref=part,
             dst_ref=part,
             send_sem=ag_send.at[layer, j, k],
             recv_sem=ag_recv.at[layer, j, k],
-            device_id={"rep": (mr + k) % n_rep},
+            device_id={"rep": to},
             device_id_type=MESH,
         )
 
     def pb_copy(j, k):
-        to = (mr + k) % n_rep
+        to = (near, near, far)[k]
+        src = (pbs.at[near], pbs.at[near_far], pair)[k]
         return pltpu.make_async_remote_copy(
-            src_ref=pbs.at[to, block(j)],
+            src_ref=src.at[block(j)],
             dst_ref=pbr.at[k, block(j)],
             send_sem=pb_send.at[j, k],
             recv_sem=pb_recv.at[j, k],
             device_id={"rep": to},
             device_id_type=MESH,
         )
+
+    def pb_pair(j):
+        pb_copy(j, 0).wait_recv()
+        pb_copy(j, 1).wait_recv()
+        both = pbs[far, block(j)].astype(F32) + pbr[1, block(j)].astype(F32)
+        pair[block(j)] = both.astype(BF)
+        pb_copy(j, 2).start()
+
+    def pass_on(layer, j):
+        if j < rows:
+            ag_copy(layer, j, 1).wait_recv()
+            ag_copy(layer, j, 2).start()
 
     def is_type(j, t):
         return (types[:, j : j + 1] == t).astype(F32)
@@ -171,12 +189,15 @@
         full = (agg1, agg2)[layer]
         there = dot(spread_halo[block(j)], halo[layer, pl.ds(0, n_dom * cap)])
         full[block(j), own_cols(mr)] = (local + there).astype(BF)
-        for k in range(1, n_rep):
-            ag_copy(layer, j, k).start()
+        ag_copy(layer, j, 1).start()
+        ag_copy(layer, j, 0).start()
 
     def expert(layer, j):
-        for k in range(1, n_rep):
-            ag_copy(layer, j, k).wait_recv()
+        if j == 0:
+            pass_on(layer, 0)
+        pass_on(layer, j + 1)
+        ag_copy(layer, j, 0).wait_recv()
+        ag_copy(layer, j, 2).wait_recv()
         return dot((agg1, agg2)[layer][block(j)], chosen[layer, j])
 
     def spread_types(j, dz):
@@ -212,10 +233,13 @@
         back = dot(dz.astype(BF), chosen[1, j], ((1,), (1,))).astype(BF)
         for r in range(n_rep):
             pbs[r, block(j)] = back[:, r * cols : (r + 1) * cols]
-        for k in range(1, n_rep):
-            pb_copy(j, k).start()
+        pb_copy(j, 0).start()
+        pb_copy(j, 1).start()
         spread_types(j, dz)
         h2_out[block(j)] = (h1_out[block(j)].astype(F32) + z * sigmoid(z)).astype(BF)
+        if j > 0:
+            pb_pair(j - 1)
+    pb_pair(rows - 1)
 
     orders = bit_orders(n_dom)
     streams = len(orders)
@@ -324,11 +348,9 @@
         copy.start()
     rs_begin(1)
     for j in range(rows):
-        for k in range(1, n_rep):
-            pb_copy(j, k).wait_recv()
-        total = pbs[mr, block(j)].astype(F32)
-        for k in range(1, n_rep):
-            total = total + pbr[k, block(j)].astype(F32)
+        pb_copy(j, 2).wait_recv()
+        total = pbs[mr, block(j)].astype(F32) + pbr[0, block(j)].astype(F32)
+        total = total + pbr[2, block(j)].astype(F32)
         dh = gout[block(j)].astype(F32) + dot(lval[block(j)], total.astype(BF), ((0,), (0,)))
         spread_types(j, dh * slope_silu(z1s[block(j)]))
 
@@ -345,7 +367,7 @@
     for layer in range(2):
         loop_picks(layer, lambda copy: copy.wait_send())
         for j in range(rows):
-            for k in range(1, n_rep):
+            for k in range(3):
                 ag_copy(layer, j, k).wait_send()
         for q in range(streams):
             for s in range(depth):
@@ -355,16 +377,24 @@
     for copy in writes:
         copy.wait()
     for j in range(rows):
-        for k in range(1, n_rep):
+        for k in range(3):
             pb_copy(j, k).wait_send()
 
 
-def write_back(h2, h1, g1, g2, h2_out, h1_out, g1_out, g2_out, sem):
-    pairs = ((g1, g1_out), (g2, g2_out), (h1, h1_out), (h2, h2_out))
-    copies = [pltpu.make_async_copy(a, b, sem.at[n]) for n, (a, b) in enumerate(pairs)]
-    for copy in copies:
+def write_back(h2, h1, g1, g2, h2_out, h1_out, g1_out, g2_out, h2_in, h1_in, g1_in, g2_in, sem):
+    pieces = [(h1, h1_in, h1_out), (h2, h2_in, h2_out)]
+    part = g1.shape[0] // 4
+    for here in [pl.ds(n * part, part) for n in range(4)]:
+        pieces.append((g1.at[here], g1_in.at[here], g1_out.at[here]))
+        pieces.append((g2.at[here], g2_in.at[here], g2_out.at[here]))
+    into = [pltpu.make_async_copy(a, b, sem.at[0, n]) for n, (a, b, _) in enumerate(pieces)]
+    back = [pltpu.make_async_copy(b, c, sem.at[1, n]) for n, (_, b, c) in enumerate(pieces)]
+    for copy in into:
         copy.start()
-    for copy in copies:
+    for first, second in zip(into, back):
+        first.wait()
+        second.start()
+    for copy in back:
         copy.wait()
 
 
@@ -412,7 +442,8 @@
             pltpu.VMEM((nodes, width), BF),
             pltpu.VMEM((nodes, width), BF),
             pltpu.VMEM((n_rep, nodes, cols), BF),
-            pltpu.VMEM((n_rep, nodes, cols), BF),
+            pltpu.VMEM((3, nodes, cols), BF),
+            pltpu.VMEM((nodes, cols), BF),
             pltpu.VMEM((nodes, cols), F32),
             pltpu.VMEM((nodes, experts * cols), BF),
             pltpu.VMEM((nodes, n_dom * cap), BF),
@@ -445,7 +476,8 @@
         out_shape=tuple(jax.ShapeDtypeStruct(a.shape, a.dtype) for a in (h_two, h_one, g_one, g_two)),
         in_specs=[pl.BlockSpec(memory_space=pl.ANY)] * 4,
         out_specs=(hbm,) * 4,
-        scratch_shapes=[dma((4,))],
+        scratch_shapes=[pltpu.VMEM(a.shape, a.dtype) for a in (h_two, h_one, g_one, g_two)]
+        + [dma((2, 10))],
         compiler_params=pltpu.CompilerParams(vmem_limit_bytes=VMEM_LIMIT),
     )(h_two, h_one, g_one, g_two)
 

time: 220 us -> 87.2 us (0.40)
  Pallas kernels: 220 us -> 86.4 us
    pallas_call x1, Pallas kernels: 136 us -> 4.06 us  [shards(): pl.pallas_call(write_back, out_shape=tuple((jax.ShapeDtypeStruct(a.shape,...]
where the time goes in v4:
time: 87.2 us; the launch traced here: 87 us
  Pallas kernels  86.4 us (99%)
    pallas_call x1, Pallas kernels, shards(): pl.pallas_call(functools.partial(step_kernel, n_dom, n_rep, cap, tile), o...  82.3 us
    pallas_call x1, Pallas kernels, shards(): pl.pallas_call(write_back, out_shape=tuple((jax.ShapeDtypeStruct(a.shape,...  4.06 us

profile of v4, /device:TPU:0, one launch (start us, length us, event | category | flops | bytes accessed | tf_op | source)
XLA Modules:
  0.0 87.0 jit_solution(6021494662490900718)
XLA Ops:
  0.6 82.3 %shard_map.129 = (bf16[512,128]{1,0:T(8,128)(2,1)}, bf16[512,128]{1,0:T(8,128)(2,1)}, f32[4096,128]{1,0:T(8,128)}, f32[4096,128]{1,0:T(8,128)}) custom-call(bf16[512,128]{1,0:T(8,128)(2,1)} %feats_in.1, bf16[512,128]{1,0:T(8,128)(2,1)} %hist_in.1, bf16[512,128]{1,0:T(8,128)(2,1)} %lval_in.1, bf16[512,128]{1,0:T(8,128)(2,1)} %hval_in.1, s32[8,64]{1,0:T(8,128)} %bitcast.3, ...), custom_call_target="tpu_custom_call" | custom-call | tf_op jit(solution)/shard_map/pallas_call | solution.py:423
  83.0 4.1 %shard_map.130 = (bf16[512,128]{1,0:T(8,128)(2,1)}, bf16[512,128]{1,0:T(8,128)(2,1)}, f32[4096,128]{1,0:T(8,128)}, f32[4096,128]{1,0:T(8,128)}) custom-call(bf16[512,128]{1,0:T(8,128)(2,1)} %get-tuple-element.12.h2, bf16[512,128]{1,0:T(8,128)(2,1)} %get-tuple-element.13.h1, f32[4096,128]{1,0:T(8,128)} %get-tuple-element.14.g1, f32[4096,128]{1,0:T(8,128)} %get-tuple-element.15.g2), custom_call_target="tpu_custom_call" | custom-call | tf_op jit(solution)/shard_map/pallas_call | solution.py:474

commit v5 on v4

--- a/solution.py
+++ b/solution.py
@@ -37,7 +37,7 @@
     feats_in, hist_in, lval_in, hval_in, picks_in, htile_in, types_in, w1_in, w2_in, gout_in,
     h2_hbm, h1_hbm, g1_hbm, g2_hbm,
     h2_out, h1_out, g1_out, g2_out, out_sem, grad_sem,
-    picked, halo, agg1, agg2, pbs, pbr, pair, z1s, dzm, spread_halo, acc, sbuf, rbuf, res, wide, chosen,
+    picked, halo, agg1, agg2, pbs, pbr, pair, summed, z1s, dzm, spread_halo, acc, sbuf, rbuf, res, wide, chosen,
     feats, hist, lval, hval, picks, htile, types, w1, w2, gout, onehot, in_sem,
     pick_send, pick_recv, ag_send, ag_recv, pb_send, pb_recv, rs_send, rs_recv, gat_send, gat_recv,
 ):
@@ -120,6 +120,15 @@
     def block(j):
         return pl.ds(j * tile, tile)
 
+    groups = rows // 2 if rows % 2 == 0 else rows
+    members = rows // groups
+
+    def group(g):
+        return pl.ds(g * members * tile, members * tile)
+
+    def per_block(g, product):
+        return jnp.concatenate([product(j) for j in range(g * members, (g + 1) * members)])
+
     def own_cols(r):
         return pl.ds(pl.multiple_of(r * cols, cols), cols)
 
@@ -129,7 +138,7 @@
 
     def ag_copy(layer, j, k):
         held, to = ((mr, near), (mr, far), (far, near))[k]
-        part = (agg1, agg2)[layer].at[block(j), own_cols(held)]
+        part = (agg1, agg2)[layer].at[group(j), own_cols(held)]
         return pltpu.make_async_remote_copy(
             src_ref=part,
             dst_ref=part,
@@ -143,8 +152,8 @@
         to = (near, near, far)[k]
         src = (pbs.at[near], pbs.at[near_far], pair)[k]
         return pltpu.make_async_remote_copy(
-            src_ref=src.at[block(j)],
-            dst_ref=pbr.at[k, block(j)],
+            src_ref=src.at[group(j)],
+            dst_ref=pbr.at[k, group(j)],
             send_sem=pb_send.at[j, k],
             recv_sem=pb_recv.at[j, k],
             device_id={"rep": to},
@@ -154,12 +163,12 @@
     def pb_pair(j):
         pb_copy(j, 0).wait_recv()
         pb_copy(j, 1).wait_recv()
-        both = pbs[far, block(j)].astype(F32) + pbr[1, block(j)].astype(F32)
-        pair[block(j)] = both.astype(BF)
+        both = pbs[far, group(j)].astype(F32) + pbr[1, group(j)].astype(F32)
+        pair[group(j)] = both.astype(BF)
         pb_copy(j, 2).start()
 
     def pass_on(layer, j):
-        if j < rows:
+        if j < groups:
             ag_copy(layer, j, 1).wait_recv()
             ag_copy(layer, j, 2).start()
 
@@ -187,8 +196,8 @@
 
     def aggregate(layer, j, local):
         full = (agg1, agg2)[layer]
-        there = dot(spread_halo[block(j)], halo[layer, pl.ds(0, n_dom * cap)])
-        full[block(j), own_cols(mr)] = (local + there).astype(BF)
+        there = dot(spread_halo[group(j)], halo[layer, pl.ds(0, n_dom * cap)])
+        full[group(j), own_cols(mr)] = (local + there).astype(BF)
         ag_copy(layer, j, 1).start()
         ag_copy(layer, j, 0).start()
 
@@ -198,7 +207,7 @@
         pass_on(layer, j + 1)
         ag_copy(layer, j, 0).wait_recv()
         ag_copy(layer, j, 2).wait_recv()
-        return dot((agg1, agg2)[layer][block(j)], chosen[layer, j])
+        return per_block(j, lambda b: dot((agg1, agg2)[layer][block(b)], chosen[layer, b]))
 
     def spread_types(j, dz):
         for t in range(experts):
@@ -211,35 +220,39 @@
             held = (htile[:, j : j + 1] == b).astype(F32)
             spread_halo[block(j), b * tile : (b + 1) * tile] = (own_tile * held).astype(BF)
     unpack_weights(0)
-    local = [dot(lval[block(j)], feats[block(j)]) for j in range(rows)]
+    local = [per_block(g, lambda j: dot(lval[block(j)], feats[block(j)])) for g in range(groups)]
     loop_picks(0, lambda copy: copy.wait_recv())
     compact(0)
-    for j in range(rows):
-        aggregate(0, j, local[j])
+    for g in range(groups):
+        aggregate(0, g, local[g])
     ready(w2)
     unpack_weights(1)
     ready(gout)
     loop_picks(1, lambda copy: copy.wait_recv())
     compact(1)
-    for j in range(rows):
-        z = expert(0, j)
-        h = (feats[block(j)].astype(F32) + z * sigmoid(z)).astype(BF)
-        z1s[block(j)] = z
-        h1_out[block(j)] = h
-        aggregate(1, j, dot(lval[block(j)], h))
-    for j in range(rows):
-        z = expert(1, j)
-        dz = gout[block(j)].astype(F32) * slope_silu(z)
-        back = dot(dz.astype(BF), chosen[1, j], ((1,), (1,))).astype(BF)
+    for g in range(groups):
+        z = expert(0, g)
+        z1s[group(g)] = z
+        h1_out[group(g)] = (feats[group(g)].astype(F32) + z * sigmoid(z)).astype(BF)
+        aggregate(1, g, per_block(g, lambda j: dot(lval[block(j)], h1_out[block(j)])))
+    for g in range(groups):
+        z = expert(1, g)
+        dz = gout[group(g)].astype(F32) * slope_silu(z)
+        first = g * members
+        parts = [dz[n * tile : (n + 1) * tile] for n in range(members)]
+        back = per_block(
+            g, lambda j: dot(parts[j - first].astype(BF), chosen[1, j], ((1,), (1,)))
+        ).astype(BF)
         for r in range(n_rep):
-            pbs[r, block(j)] = back[:, r * cols : (r + 1) * cols]
-        pb_copy(j, 0).start()
-        pb_copy(j, 1).start()
-        spread_types(j, dz)
-        h2_out[block(j)] = (h1_out[block(j)].astype(F32) + z * sigmoid(z)).astype(BF)
-        if j > 0:
-            pb_pair(j - 1)
-    pb_pair(rows - 1)
+            pbs[r, group(g)] = back[:, r * cols : (r + 1) * cols]
+        pb_copy(g, 0).start()
+        pb_copy(g, 1).start()
+        for n in range(members):
+            spread_types(first + n, parts[n])
+        h2_out[group(g)] = (h1_out[group(g)].astype(F32) + z * sigmoid(z)).astype(BF)
+        if g > 0:
+            pb_pair(g - 1)
+    pb_pair(groups - 1)
 
     orders = bit_orders(n_dom)
     streams = len(orders)
@@ -347,12 +360,14 @@
     for copy in writes:
         copy.start()
     rs_begin(1)
-    for j in range(rows):
-        pb_copy(j, 2).wait_recv()
-        total = pbs[mr, block(j)].astype(F32) + pbr[0, block(j)].astype(F32)
-        total = total + pbr[2, block(j)].astype(F32)
-        dh = gout[block(j)].astype(F32) + dot(lval[block(j)], total.astype(BF), ((0,), (0,)))
-        spread_types(j, dh * slope_silu(z1s[block(j)]))
+    for g in range(groups):
+        pb_copy(g, 2).wait_recv()
+        total = pbs[mr, group(g)].astype(F32) + pbr[0, group(g)].astype(F32)
+        summed[group(g)] = (total + pbr[2, group(g)].astype(F32)).astype(BF)
+        back = per_block(g, lambda j: dot(lval[block(j)], summed[block(j)], ((0,), (0,))))
+        dz = (gout[group(g)].astype(F32) + back) * slope_silu(z1s[group(g)])
+        for n in range(members):
+            spread_types(g * members + n, dz[n * tile : (n + 1) * tile])
 
     rs_begin(0)
     steps = [(rs_step, s) for s in range(depth)] + [(gat_step, s) for s in reversed(range(depth))]
@@ -366,7 +381,7 @@
 
     for layer in range(2):
         loop_picks(layer, lambda copy: copy.wait_send())
-        for j in range(rows):
+        for j in range(groups):
             for k in range(3):
                 ag_copy(layer, j, k).wait_send()
         for q in range(streams):
@@ -376,7 +391,7 @@
             grad_write(layer, q).wait()
     for copy in writes:
         copy.wait()
-    for j in range(rows):
+    for j in range(groups):
         for k in range(3):
             pb_copy(j, k).wait_send()
 
@@ -444,6 +459,7 @@
             pltpu.VMEM((n_rep, nodes, cols), BF),
             pltpu.VMEM((3, nodes, cols), BF),
             pltpu.VMEM((nodes, cols), BF),
+            pltpu.VMEM((nodes, cols), BF),
             pltpu.VMEM((nodes, cols), F32),
             pltpu.VMEM((nodes, experts * cols), BF),
             pltpu.VMEM((nodes, n_dom * cap), BF),

time: 87.2 us -> 85.5 us (0.981)
  Pallas kernels: 86.4 us -> 84.7 us
    pallas_call x1, Pallas kernels: 82.3 us -> 80.6 us  [shards(): pl.pallas_call(functools.partial(step_kernel, n_dom, n_rep, cap, tile), o...]
where the time goes in v5:
time: 85.5 us; the launch traced here: 85.3 us
  Pallas kernels  84.7 us (99%)
    pallas_call x1, Pallas kernels, shards(): pl.pallas_call(functools.partial(step_kernel, n_dom, n_rep, cap, tile), o...  80.6 us
    pallas_call x1, Pallas kernels, shards(): pl.pallas_call(write_back, out_shape=tuple((jax.ShapeDtypeStruct(a.shape,...  4.06 us

profile of v5, /device:TPU:0, one launch (start us, length us, event | category | flops | bytes accessed | tf_op | source)
XLA Modules:
  0.0 85.3 jit_solution(16254954454713268006)
XLA Ops:
  0.6 80.6 %shard_map.129 = (bf16[512,128]{1,0:T(8,128)(2,1)}, bf16[512,128]{1,0:T(8,128)(2,1)}, f32[4096,128]{1,0:T(8,128)}, f32[4096,128]{1,0:T(8,128)}) custom-call(bf16[512,128]{1,0:T(8,128)(2,1)} %feats_in.1, bf16[512,128]{1,0:T(8,128)(2,1)} %hist_in.1, bf16[512,128]{1,0:T(8,128)(2,1)} %lval_in.1, bf16[512,128]{1,0:T(8,128)(2,1)} %hval_in.1, s32[8,64]{1,0:T(8,128)} %bitcast.3, ...), custom_call_target="tpu_custom_call" | custom-call | tf_op jit(solution)/shard_map/pallas_call | solution.py:438
  81.3 4.1 %shard_map.130 = (bf16[512,128]{1,0:T(8,128)(2,1)}, bf16[512,128]{1,0:T(8,128)(2,1)}, f32[4096,128]{1,0:T(8,128)}, f32[4096,128]{1,0:T(8,128)}) custom-call(bf16[512,128]{1,0:T(8,128)(2,1)} %get-tuple-element.12.h2, bf16[512,128]{1,0:T(8,128)(2,1)} %get-tuple-element.13.h1, f32[4096,128]{1,0:T(8,128)} %get-tuple-element.14.g1, f32[4096,128]{1,0:T(8,128)} %get-tuple-element.15.g2), custom_call_target="tpu_custom_call" | custom-call | tf_op jit(solution)/shard_map/pallas_call | solution.py:490

commit v6 on v5

--- a/solution.py
+++ b/solution.py
@@ -37,7 +37,7 @@
     feats_in, hist_in, lval_in, hval_in, picks_in, htile_in, types_in, w1_in, w2_in, gout_in,
     h2_hbm, h1_hbm, g1_hbm, g2_hbm,
     h2_out, h1_out, g1_out, g2_out, out_sem, grad_sem,
-    picked, halo, agg1, agg2, pbs, pbr, pair, summed, z1s, dzm, spread_halo, acc, sbuf, rbuf, res, wide, chosen,
+    picked, halo, agg1, agg2, pbs, pbr, pair, summed, z2s, z1s, dzm, spread_halo, acc, sbuf, rbuf, res, wide, chosen,
     feats, hist, lval, hval, picks, htile, types, w1, w2, gout, onehot, in_sem,
     pick_send, pick_recv, ag_send, ag_recv, pb_send, pb_recv, rs_send, rs_recv, gat_send, gat_recv,
 ):
@@ -104,9 +104,12 @@
         lax.fori_loop(1, n_dom, body, 0)
 
     own = pl.ds(pl.multiple_of(me * pad, pad), pad)
-    for layer in range(2):
+
+    def send_picks(layer):
         loop_picks(layer, lambda copy: copy.start())
         halo[layer, own] = picked[layer, own]
+
+    send_picks(0)
 
     def compact(layer):
         if pad == cap:
@@ -225,6 +228,7 @@
     compact(0)
     for g in range(groups):
         aggregate(0, g, local[g])
+    send_picks(1)
     ready(w2)
     unpack_weights(1)
     ready(gout)
@@ -249,7 +253,7 @@
         pb_copy(g, 1).start()
         for n in range(members):
             spread_types(first + n, parts[n])
-        h2_out[group(g)] = (h1_out[group(g)].astype(F32) + z * sigmoid(z)).astype(BF)
+        z2s[group(g)] = z
         if g > 0:
             pb_pair(g - 1)
     pb_pair(groups - 1)
@@ -357,9 +361,10 @@
         pltpu.make_async_copy(h1_out, h1_hbm, out_sem.at[0]),
         pltpu.make_async_copy(h2_out, h2_hbm, out_sem.at[1]),
     )
+    rs_begin(1)
+    h2_out[...] = (h1_out[...].astype(F32) + z2s[...] * sigmoid(z2s[...])).astype(BF)
     for copy in writes:
         copy.start()
-    rs_begin(1)
     for g in range(groups):
         pb_copy(g, 2).wait_recv()
         total = pbs[mr, group(g)].astype(F32) + pbr[0, group(g)].astype(F32)
@@ -461,6 +466,7 @@
             pltpu.VMEM((nodes, cols), BF),
             pltpu.VMEM((nodes, cols), BF),
             pltpu.VMEM((nodes, cols), F32),
+            pltpu.VMEM((nodes, cols), F32),
             pltpu.VMEM((nodes, experts * cols), BF),
             pltpu.VMEM((nodes, n_dom * cap), BF),
             pltpu.VMEM((2, streams, length, cols), F32),

time: 85.5 us -> 89 us (1.041)
  Pallas kernels: 84.7 us -> 88.1 us
    pallas_call x1, Pallas kernels: 80.6 us -> 84.1 us  [shards(): pl.pallas_call(functools.partial(step_kernel, n_dom, n_rep, cap, tile), o...]
where the time goes in v6:
time: 89 us; the launch traced here: 88.8 us
  Pallas kernels  88.1 us (99%)
    pallas_call x1, Pallas kernels, shards(): pl.pallas_call(functools.partial(step_kernel, n_dom, n_rep, cap, tile), o...  84.1 us
    pallas_call x1, Pallas kernels, shards(): pl.pallas_call(write_back, out_shape=tuple((jax.ShapeDtypeStruct(a.shape,...  4.06 us

profile of v6, /device:TPU:0, one launch (start us, length us, event | category | flops | bytes accessed | tf_op | source)
XLA Modules:
  0.0 88.8 jit_solution(30437659011859076)
XLA Ops:
  0.6 84.1 %shard_map.129 = (bf16[512,128]{1,0:T(8,128)(2,1)}, bf16[512,128]{1,0:T(8,128)(2,1)}, f32[4096,128]{1,0:T(8,128)}, f32[4096,128]{1,0:T(8,128)}) custom-call(bf16[512,128]{1,0:T(8,128)(2,1)} %feats_in.1, bf16[512,128]{1,0:T(8,128)(2,1)} %hist_in.1, bf16[512,128]{1,0:T(8,128)(2,1)} %lval_in.1, bf16[512,128]{1,0:T(8,128)(2,1)} %hval_in.1, s32[8,64]{1,0:T(8,128)} %bitcast.3, ...), custom_call_target="tpu_custom_call" | custom-call | tf_op jit(solution)/shard_map/pallas_call | solution.py:443
  84.7 4.1 %shard_map.130 = (bf16[512,128]{1,0:T(8,128)(2,1)}, bf16[512,128]{1,0:T(8,128)(2,1)}, f32[4096,128]{1,0:T(8,128)}, f32[4096,128]{1,0:T(8,128)}) custom-call(bf16[512,128]{1,0:T(8,128)(2,1)} %get-tuple-element.12.h2, bf16[512,128]{1,0:T(8,128)(2,1)} %get-tuple-element.13.h1, f32[4096,128]{1,0:T(8,128)} %get-tuple-element.14.g1, f32[4096,128]{1,0:T(8,128)} %get-tuple-element.15.g2), custom_call_target="tpu_custom_call" | custom-call | tf_op jit(solution)/shard_map/pallas_call | solution.py:496
